TPU v7x, 32 devices: a whole 2x2x4 slice. The times are simulated.
32 devices in a mesh: seq: 16 (over z, x, core), head: 2 (over y).
Axes of the slice: x: 2, y: 2, z: 4, core: 2. Of those that a mesh axis runs over, the one named last changes fastest.
Arguments:
- queries: bfloat16 [2048, 1024], P('seq', 'head'), may hold values from -8 to 8
- keys: bfloat16 [2048, 1024], P('seq', 'head'), may hold values from -8 to 8
- values: bfloat16 [2048, 1024], P('seq', 'head'), may hold values from -8 to 8
- w_out: bfloat16 [1024, 1024], P('head'), may hold values from -0.1875 to 0.1875
- d_mixed: bfloat16 [2048, 1024], P('seq'), may hold values from -6 to 6
Outputs:
- mixed: bfloat16 [2048, 1024], P(('seq', 'head'))
- d_queries: bfloat16 [2048, 1024], P('seq', 'head')
- d_keys: bfloat16 [2048, 1024], P('seq', 'head')
- d_values: bfloat16 [2048, 1024], P('seq', 'head')
All inputs are finite; a program needn't handle non-finite values.
Results may differ from a plain program's by a relative error of at most 0.0074.
Values may be sent and summed in bfloat16 or wider, within the bound.
A program may use at most 64 MiB of HBM per device.

v0:
```python
import math

import jax
import jax.numpy as jnp
from jax import lax
from jax.sharding import PartitionSpec as P

HEAD_DIM = 64
BLOCK = 64


def with_halo(cells, sides, width):
    for axis, dim in sides:
        count = lax.axis_size(axis)
        ends = count - 1
        head = lax.slice_in_dim(cells, 0, width, axis=dim)
        tail = lax.slice_in_dim(cells, cells.shape[dim] - width, cells.shape[dim], axis=dim)
        cells = jnp.concatenate(
            [
                lax.ppermute(tail, axis, [(i, (i + 1) % count) for i in range(ends)]),
                cells,
                lax.ppermute(head, axis, [((i + 1) % count, i) for i in range(ends)]),
            ],
            axis=dim,
        )
    return cells


def swapped(value, axis, apart):
    mask = 2**apart
    pairs = [(source, source ^ mask) for source in range(lax.axis_size(axis))]
    return lax.ppermute(value, axis, pairs)


def score_product(form, left, right):
    return jnp.einsum(form, left, right, preferred_element_type=jnp.float32)


def fine_sets(source, row_share, block_length):
    count_of_blocks = row_share // block_length
    feature_share = source.shape[1]
    return jnp.concatenate(
        [
            source[:row_share].reshape(count_of_blocks, block_length, feature_share),
            source[block_length : block_length + row_share].reshape(
                count_of_blocks, block_length, feature_share
            ),
            source[2 * block_length :].reshape(count_of_blocks, block_length, feature_share),
        ],
        axis=1,
    )


def key_sets(source, far_source, block_length):
    row_share = source.shape[0] - 2 * block_length
    count_of_blocks = row_share // block_length
    feature_share = source.shape[1]
    target = [fine_sets(source, row_share, block_length)]
    far_flat = far_source.astype(jnp.bfloat16).reshape(-1, feature_share)
    target.append(
        jnp.broadcast_to(far_flat[None], (count_of_blocks, far_flat.shape[0], feature_share))
    )
    return jnp.concatenate(target, axis=1)


def return_scatter(grad_sets, row_share, block_length):
    count_of_blocks, total_key_count, feature_share = grad_sets.shape
    grad_rows = jnp.pad(
        grad_sets[:, :block_length].reshape(row_share, feature_share),
        ((0, 2 * block_length), (0, 0)),
    )
    grad_rows = grad_rows + jnp.pad(
        grad_sets[:, block_length : 2 * block_length].reshape(row_share, feature_share),
        ((block_length, block_length), (0, 0)),
    )
    grad_rows = grad_rows + jnp.pad(
        grad_sets[:, 2 * block_length : 3 * block_length].reshape(row_share, feature_share),
        ((2 * block_length, 0), (0, 0)),
    )
    central_extra = jnp.zeros((row_share, feature_share), jnp.float32)
    offset = 3 * block_length
    far_grad = grad_sets[:, offset:].sum(axis=0).reshape(-1, block_length, feature_share)
    grad_rows = grad_rows + jnp.pad(central_extra, ((block_length, block_length), (0, 0)))
    return (grad_rows, far_grad)


def attend(
    query_rows,
    keys_ext,
    values_ext,
    far_keys,
    far_values,
    grad_attn,
    at_start,
    at_end,
    block_length,
    head_dim,
):
    row_share, feature_share = query_rows.shape
    count_of_blocks = row_share // block_length
    head_count = feature_share // head_dim
    key_all = key_sets(keys_ext, far_keys, block_length)
    value_all = key_sets(values_ext, far_values, block_length)
    total_key_count = key_all.shape[1]
    query_blocks = query_rows.reshape(count_of_blocks, block_length, head_count, head_dim)
    key_blocks = key_all.reshape(count_of_blocks, total_key_count, head_count, head_dim)
    value_blocks = value_all.reshape(count_of_blocks, total_key_count, head_count, head_dim)
    inv_scale = 1.0 / math.sqrt(head_dim)
    scores = score_product("nqhd,nkhd->nhqk", query_blocks, key_blocks) * inv_scale
    column = lax.broadcasted_iota(jnp.int32, (count_of_blocks, total_key_count), 1)
    block_ids = lax.broadcasted_iota(jnp.int32, (count_of_blocks, total_key_count), 0)
    blocked = (block_ids == 0) & (column < block_length) & at_start | (
        block_ids == count_of_blocks - 1
    ) & (column >= 2 * block_length) & (column < 3 * block_length) & at_end
    scores = jnp.where(blocked[:, None, None, :], -jnp.inf, scores)
    row_max = jnp.max(scores, axis=-1, keepdims=True)
    exp_terms = jnp.exp(scores - row_max)
    normed = exp_terms / jnp.sum(exp_terms, axis=-1, keepdims=True)
    softmax_weights = normed.astype(jnp.bfloat16)
    attention_layer = (
        score_product("nhqk,nkhd->nqhd", softmax_weights, value_blocks)
        .reshape(row_share, feature_share)
        .astype(jnp.bfloat16)
    )
    gradient_blocks = grad_attn.reshape(count_of_blocks, block_length, head_count, head_dim)
    grad_normed = score_product("nqhd,nkhd->nhqk", gradient_blocks, value_blocks)
    inner_sum = jnp.sum(normed * grad_normed, axis=-1, keepdims=True)
    grad_scores = (normed * (grad_normed - inner_sum) * inv_scale).astype(jnp.bfloat16)
    query_gradient = score_product("nhqk,nkhd->nqhd", grad_scores, key_blocks).reshape(
        row_share, feature_share
    )
    grad_kset = score_product("ueji,ujeo->uieo", grad_scores, query_blocks).reshape(
        count_of_blocks, total_key_count, feature_share
    )
    value_set_gradient = score_product("ueji,ujeo->uieo", softmax_weights, gradient_blocks).reshape(
        count_of_blocks, total_key_count, feature_share
    )
    extended_key_gradient, remote_key_gradient = return_scatter(grad_kset, row_share, block_length)
    extended_value_gradient, remote_value_gradient = return_scatter(
        value_set_gradient, row_share, block_length
    )
    return (
        attention_layer,
        query_gradient,
        extended_key_gradient,
        extended_value_gradient,
        remote_key_gradient,
        remote_value_gradient,
    )


def pool_pair(sets):
    return jnp.mean(sets.reshape(sets.shape[0], sets.shape[1] // 2, 2, sets.shape[2]), axis=2)


def spread_pair(sets):
    return jnp.repeat(sets, 2, axis=1) * 0.5


def on_device(queries, keys, values, w_out, d_mixed):
    row_share, feature_share = queries.shape
    block_length = BLOCK
    seq_place = lax.axis_index("seq")
    devices = lax.axis_size("seq")
    far_levels = devices.bit_length() - 1
    stacked = jnp.stack([keys, values])
    padded = with_halo(stacked, (("seq", 1),), block_length)
    own_sets = jnp.mean(
        stacked.reshape(2, block_length, row_share // block_length, feature_share),
        axis=2,
        dtype=jnp.float32,
    )
    far_list = []
    current = own_sets
    for bit_level in range(far_levels):
        partner = swapped(current, "seq", bit_level)
        far_list.append(partner)
        low_side = seq_place >> bit_level & 1 == 0
        own_half = pool_pair(current)
        other_half = pool_pair(partner)
        current = jnp.where(
            low_side,
            jnp.concatenate([own_half, other_half], axis=1),
            jnp.concatenate([other_half, own_half], axis=1),
        )
    far_stack = jnp.stack(far_list, axis=1)
    grad_attn = lax.dot_general(
        d_mixed, w_out, (((1,), (1,)), ((), ())), preferred_element_type=jnp.float32
    ).astype(jnp.bfloat16)
    layer_results = attend(
        queries,
        padded[0],
        padded[1],
        far_stack[0],
        far_stack[1],
        grad_attn,
        seq_place == 0,
        seq_place == devices - 1,
        block_length,
        HEAD_DIM,
    )
    (
        attention_layer,
        query_gradient,
        extended_key_gradient,
        extended_value_gradient,
        remote_key_gradient,
        remote_value_gradient,
    ) = layer_results
    mixed = lax.psum_scatter(
        jnp.dot(attention_layer, w_out, preferred_element_type=jnp.float32),
        "head",
        scatter_dimension=0,
        tiled=True,
    ).astype(jnp.bfloat16)
    remote_gradient = jnp.stack([remote_key_gradient, remote_value_gradient])
    upper_grad = jnp.zeros((2, block_length, feature_share), jnp.float32)
    half_len = block_length // 2
    for bit_level in reversed(range(far_levels)):
        low_side = seq_place >> bit_level & 1 == 0
        first_half = upper_grad[:, :half_len]
        second_half = upper_grad[:, half_len:]
        own_half = jnp.where(low_side, first_half, second_half)
        theirs = jnp.where(low_side, second_half, first_half)
        outgoing = remote_gradient[:, bit_level] + spread_pair(theirs)
        incoming = swapped(outgoing.astype(jnp.bfloat16), "seq", bit_level).astype(outgoing.dtype)
        upper_grad = incoming + spread_pair(own_half)
    group_len = row_share // block_length
    base_grad = jnp.broadcast_to(
        (upper_grad / group_len)[:, :, None, :], (2, block_length, group_len, feature_share)
    ).reshape(2, row_share, feature_share)
    rim_grads = jnp.stack(
        [
            jnp.concatenate(
                [
                    extended_key_gradient[:block_length],
                    extended_key_gradient[row_share + block_length :],
                ],
                axis=0,
            ),
            jnp.concatenate(
                [
                    extended_value_gradient[:block_length],
                    extended_value_gradient[row_share + block_length :],
                ],
                axis=0,
            ),
        ]
    )
    rim_back = with_halo(rim_grads.astype(jnp.bfloat16), (("seq", 1),), block_length).astype(
        rim_grads.dtype
    )
    inner_rows = (
        jnp.stack(
            [
                extended_key_gradient[block_length : block_length + row_share],
                extended_value_gradient[block_length : block_length + row_share],
            ]
        )
        + base_grad
    )
    inner_rows = inner_rows + jnp.pad(
        rim_back[:, :block_length], ((0, 0), (0, row_share - block_length), (0, 0))
    )
    inner_rows = inner_rows + jnp.pad(
        rim_back[:, 3 * block_length :], ((0, 0), (row_share - block_length, 0), (0, 0))
    )
    return (
        mixed,
        query_gradient.astype(jnp.bfloat16),
        inner_rows[0].astype(jnp.bfloat16),
        inner_rows[1].astype(jnp.bfloat16),
    )


def solution(mesh):
    in_specs = (
        P("seq", "head"),
        P("seq", "head"),
        P("seq", "head"),
        P("head", None),
        P("seq", None),
    )
    out_specs = (P(("seq", "head"), None), P("seq", "head"), P("seq", "head"), P("seq", "head"))
    return jax.shard_map(
        on_device, mesh=mesh, in_specs=in_specs, out_specs=out_specs, check_vma=False
    )
```

profile of v0, /device:TPU:0, one launch (start us, length us, event | category | flops | bytes accessed | tf_op | source)
XLA Modules:
  0.0 135.9 jit_solution(5914096871200715988)
XLA Ops:
  11.5 2.0 %collective-permute-start = (bf16[2,64,512]{2,1,0:T(8,128)(2,1)S(1)}, bf16[2,64,512]{2,1,0:T(8,128)(2,1)S(1)}, u32[]{:S(2)}, u32[]{:S(2)}) collective-permute-start(bf16[2,64,512]{2,1,0:T(8,128)(2,1)S(1)} %get-tuple-element.36), channel_id=1, source_target_pairs={{0,2},{2,4},{4,6},{6,8},{8,10},{10,12},{12,14},{14,16},{16,18},{18... | collective-permute-start | bytes 393224 | tf_op jit(solution)/shard_map/ppermute | solution.py:20
  13.4 1.3 collective-permute-start.1
  16.0 4.9 %collective-permute-start.3 = (f32[2,64,512]{2,1,0:T(8,128)S(1)}, f32[2,64,512]{2,1,0:T(8,128)S(1)}, u32[]{:S(2)}, u32[]{:S(2)}) collective-permute-start(f32[2,64,512]{2,1,0:T(8,128)S(1)} %maximum_select_fusion), channel_id=1, source_target_pairs={{0,4},{2,6},{4,0},{6,2},{8,12},{10,14},{12,8},{14,10},{16,20},{18,... | collective-permute-start | bytes 786440 | tf_op jit(solution)/shard_map/ppermute | solution.py:32
  21.2 6.9 %collective-permute-done.3 = f32[2,64,512]{2,1,0:T(8,128)S(1)} collective-permute-done((f32[2,64,512]{2,1,0:T(8,128)S(1)}, f32[2,64,512]{2,1,0:T(8,128)S(1)}, u32[]{:S(2)}, u32[]{:S(2)}) %collective-permute-start.3) | collective-permute-done | bytes 262176 | tf_op jit(solution)/shard_map/ppermute | solution.py:32
  28.4 1.6 %collective-permute-start.4 = (f32[2,64,512]{2,1,0:T(8,128)S(1)}, f32[2,64,512]{2,1,0:T(8,128)S(1)}, u32[]{:S(2)}, u32[]{:S(2)}) collective-permute-start(f32[2,64,512]{2,1,0:T(8,128)S(1)} %maximum_select_fusion.1), channel_id=1, source_target_pairs={{0,8},{2,10},{4,12},{6,14},{8,0},{10,2},{12,4},{14,6},{16,24},{18,... | collective-permute-start | bytes 786440 | tf_op jit(solution)/shard_map/ppermute | solution.py:32
  30.4 6.0 %collective-permute-done.4 = f32[2,64,512]{2,1,0:T(8,128)S(1)} collective-permute-done((f32[2,64,512]{2,1,0:T(8,128)S(1)}, f32[2,64,512]{2,1,0:T(8,128)S(1)}, u32[]{:S(2)}, u32[]{:S(2)}) %collective-permute-start.4) | collective-permute-done | bytes 262176 | tf_op jit(solution)/shard_map/ppermute | solution.py:32
  37.4 2.6 %collective-permute-start.5 = (bf16[2,64,512]{2,1,0:T(8,128)(2,1)}, bf16[2,64,512]{2,1,0:T(8,128)(2,1)}, u32[]{:S(2)}, u32[]{:S(2)}) collective-permute-start(bf16[2,64,512]{2,1,0:T(8,128)(2,1)} %maximum_select_fusion.2), channel_id=1, source_target_pairs={{0,16},{2,18},{4,20},{6,22},{8,24},{10,26},{12,28},{14,30},{16,0},... | collective-permute-start | bytes 393224 | tf_op jit(solution)/shard_map/ppermute | solution.py:32
  45.6 1.2 maximum_convert_fusion
  47.6 1.3 convert_element_type.102
  49.9 1.3 convert_element_type.103
  55.9 2.1 %fusion.34 = f32[2,8,64,448]{3,2,1,0:T(8,128)} fusion(bf16[2,64,8,64]{1,3,2,0:T(8,128)(2,1)S(1)} %copy.117, bf16[2,256,8,64]{1,3,2,0:T(8,128)(2,1)S(1)} %broadcast_in_dim.52, bf16[2,64,8,64]{1,3,2,0:T(8,128)(2,1)S(1)} %copy.104, bf16[2,64,8,64]{1,3,2,0:T(8,128)(2,1)S(1)} %copy.103, bf16[2,64,8,64]{1,3,2,0:T(8,128)(2,1)S(1)} %copy-done.16), kind=kOutput, calls=%fused_computation.47 | convolution fusion | flops 62390272 | bytes 2883584 | tf_op jit(solution)/shard_map/nqhd,nkhd->nhqk/dot_general | solution.py:36
  57.9 1.5 %fusion.18 = bf16[2,64,8,64]{1,3,2,0:T(8,128)(2,1)} fusion(bf16[2,256,8,64]{1,3,2,0:T(8,128)(2,1)S(1)} %broadcast_in_dim.52, bf16[2,64,8,64]{1,3,2,0:T(8,128)(2,1)S(1)} %copy.104, bf16[2,64,8,64]{1,3,2,0:T(8,128)(2,1)S(1)} %copy.103, bf16[2,64,8,64]{1,3,2,0:T(8,128)(2,1)S(1)} %copy-done.16, f32[2,8,64,448]{3,2,1,0:T(8,128)S(1)} %get-tuple-element.41, ...), kind=kOutput, calls=%fused_computation.20 | convolution fusion | flops 63373312 | bytes 2887680 | tf_op jit(solution)/shard_map/nhqk,nkhd->nqhd/dot_general | solution.py:36
  59.9 1.3 fusion.65
  61.3 1.2 slice_reduce_fusion
  62.4 8.8 %fusion.10 = f32[2,8,448,64]{2,3,1,0:T(8,128)S(1)} fusion(bf16[2,64,8,64]{1,3,2,0:T(8,128)(2,1)S(1)} %copy.113, f32[2,8,64,448]{3,2,1,0:T(8,128)} %fusion.34, f32[2,8,64,448]{3,2,1,0:T(8,128)} %copy-done.26, f32[2,8,64]{2,1,0:T(8,128)S(1)} %get-tuple-element.40), kind=kOutput, calls=%fused_computation.10 | convolution fusion | flops 61932992 | bytes 5640192 | tf_op jit(solution)/shard_map/ueji,ujeo->uieo/dot_general | solution.py:36
  71.3 1.4 %fusion.64 = (f32[2,64,512]{1,2,0:T(8,128)}, f32[2,64,512]{1,2,0:T(8,128)}, f32[2,64,512]{1,2,0:T(8,128)}) fusion(f32[2,448,512]{1,2,0:T(8,128)S(1)} %bitcast.119), kind=kLoop, calls=%fused_computation.128 | loop fusion | bytes 1572864 | tf_op jit(solution)/shard_map/slice | solution.py:69
  72.7 1.2 slice_reduce_fusion.1
  74.3 1.1 fusion.70
  75.4 1.3 copy.116
  76.7 1.9 %copy.115 = f32[2,64,512]{2,1,0:T(8,128)} copy(f32[2,64,512]{1,2,0:T(8,128)} %get-tuple-element.10) | data formatting | bytes 524288 | tf_op jit(solution)/shard_map/slice | solution.py:73
  80.8 2.1 %fusion.62 = (bf16[256,512]{1,0:T(8,128)(2,1)S(1)}, f32[256,512]{1,0:T(8,128)S(1)}, bf16[256,512]{1,0:T(8,128)(2,1)S(1)}, f32[256,512]{1,0:T(8,128)}) fusion(f32[256]{0:T(256)S(1)} %pad.38, f32[128,512]{1,0:T(8,128)S(1)} %bitcast.125, f32[128,512]{1,0:T(8,128)} %bitcast.126, f32[128,512]{1,0:T(8,128)} %bitcast.127, f32[128,512]{1,0:T(8,128)} %bitcast.128, ...), kind=kLoop, calls=%fused_computation.126 | loop fusion | flops 1048576 | bytes 3146752 | tf_op jit(solution)/shard_map/convert.13
  83.8 1.3 collective-permute-start.11
  85.1 3.7 %collective-permute-start.10 = (bf16[2,64,512]{2,1,0:T(8,128)(2,1)}, bf16[2,64,512]{2,1,0:T(8,128)(2,1)}, u32[]{:S(2)}, u32[]{:S(2)}) collective-permute-start(bf16[2,64,512]{2,1,0:T(8,128)(2,1)} %get-tuple-element.28), channel_id=1, source_target_pairs={{0,2},{2,4},{4,6},{6,8},{8,10},{10,12},{12,14},{14,16},{16,18},{18... | collective-permute-start | bytes 393224 | tf_op jit(solution)/shard_map/ppermute | solution.py:20
  90.0 1.7 %slice_bitcast_fusion = f32[1,128,512]{2,1,0:T(8,128)} fusion(f32[256,512]{1,0:T(8,128)} %get-tuple-element.39), kind=kLoop, calls=%fused_computation.62 | loop fusion | bytes 524288 | tf_op jit(solution)/shard_map/stack | solution.py:254
  91.7 7.3 %collective-permute-done.6 = bf16[2,64,512]{2,1,0:T(8,128)(2,1)S(1)} collective-permute-done((bf16[2,64,512]{2,1,0:T(8,128)(2,1)S(1)}, bf16[2,64,512]{2,1,0:T(8,128)(2,1)S(1)}, u32[]{:S(2)}, u32[]{:S(2)}) %collective-permute-start.6) | collective-permute-done | bytes 131104 | tf_op jit(solution)/shard_map/ppermute | solution.py:32
  100.3 4.7 %collective-permute-done.7 = bf16[2,64,512]{2,1,0:T(8,128)(2,1)S(1)} collective-permute-done((bf16[2,64,512]{2,1,0:T(8,128)(2,1)S(1)}, bf16[2,64,512]{2,1,0:T(8,128)(2,1)S(1)}, u32[]{:S(2)}, u32[]{:S(2)}) %collective-permute-start.7) | collective-permute-done | bytes 131104 | tf_op jit(solution)/shard_map/ppermute | solution.py:32
  106.0 1.6 %collective-permute-start.8 = (bf16[2,64,512]{2,1,0:T(8,128)(2,1)}, bf16[2,64,512]{2,1,0:T(8,128)(2,1)}, u32[]{:S(2)}, u32[]{:S(2)}) collective-permute-start(bf16[2,64,512]{2,1,0:T(8,128)(2,1)} %fusion.46), channel_id=1, source_target_pairs={{0,4},{2,6},{4,0},{6,2},{8,12},{10,14},{12,8},{14,10},{16,20},{18,... | collective-permute-start | bytes 393224 | tf_op jit(solution)/shard_map/ppermute | solution.py:32
  107.6 10.6 %fusion.19 = bf16[2,64,8,64]{1,3,2,0:T(8,128)(2,1)} fusion(f32[2,8,64,448]{3,2,1,0:T(8,128)} %fusion.34, bf16[2,256,8,64]{1,3,2,0:T(8,128)(2,1)S(1)} %copy-done.2, bf16[2,64,8,64]{1,3,2,0:T(8,128)(2,1)S(1)} %copy-done.14, bf16[2,64,8,64]{1,3,2,0:T(8,128)(2,1)S(1)} %copy-done.12, bf16[2,64,8,64]{1,3,2,0:T(8,128)(2,1)} %copy-done.15, ...), kind=kOutput, calls=%fused_computation.21 | convolution fusion | flops 65668544 | bytes 4722688 | tf_op jit(solution)/shard_map/nhqk,nkhd->nqhd/dot_general | solution.py:36
  118.2 1.1 copy.112
  120.2 1.6 %maximum_convert_fusion.2 = f32[2,64,512]{2,1,0:T(8,128)} fusion(bf16[2,64,512]{2,1,0:T(8,128)(2,1)} %collective-permute-done.11, bf16[2,64,512]{2,1,0:T(8,128)(2,1)} %collective-permute-done.10, bf16[1,128,512]{2,1,0:T(8,128)(2,1)S(1)} %maximum_bitcast_fusion.1, bf16[1,128,512]{2,1,0:T(8,128)(2,1)S(1)} %maximum_bitcast_fusion), kind=kLoop, calls=%fused_computation.86 | loop fusion | flops 524288 | bytes 786432 | tf_op jit(solution)/shard_map/slice | solution.py:266
  125.4 1.2 fusion.29
  127.4 1.6 %convert_element_type.108 = bf16[64,1024]{1,0:T(8,128)(2,1)} convert(f32[64,1024]{1,0:T(8,128)} %reduce-scatter.2.cloned.1.call-done) | non-fusion elementwise | flops 65536 | bytes 393216 | tf_op jit(solution)/shard_map/convert_element_type | solution.py:215
  (163 shorter events, 31.5 us)
Async XLA Ops:
  7.2 7.9 %copy-start = (bf16[512,1024]{1,0:T(8,128)(2,1)S(1)}, bf16[512,1024]{1,0:T(8,128)(2,1)}, u32[]{:S(2)}) copy-start(bf16[512,1024]{1,0:T(8,128)(2,1)} %param.8) | copy-start | bytes 3145732
  7.2 7.9 %copy-start.23 = (bf16[128,1024]{1,0:T(8,128)(2,1)S(1)}, bf16[128,1024]{1,0:T(8,128)(2,1)}, u32[]{:S(2)}) copy-start(bf16[128,1024]{1,0:T(8,128)(2,1)} %param.9) | copy-start | bytes 786436
  7.2 120.2 %reduce-scatter.2.cloned.1.call-start = ((), (), s32[]{:S(2)}) async-start(), calls=%async_computation.1 | async-start | bytes 786432 | tf_op jit(solution)/shard_map/reduce_scatter | solution.py:210
  10.0 5.6 %collective-permute-start.2 = (f32[2,64,512]{2,1,0:T(8,128)S(1)}, f32[2,64,512]{2,1,0:T(8,128)S(1)}, u32[]{:S(2)}, u32[]{:S(2)}) collective-permute-start(f32[2,64,512]{2,1,0:T(8,128)S(1)} %broadcast_multiply_fusion), channel_id=1, source_target_pairs={{0,2},{2,0},{4,6},{6,4},{8,10},{10,8},{12,14},{14,12},{16,18},{18,... | collective-permute-start | bytes 786440 | tf_op jit(solution)/shard_map/ppermute | solution.py:32
  11.5 30.4 %collective-permute-start = (bf16[2,64,512]{2,1,0:T(8,128)(2,1)S(1)}, bf16[2,64,512]{2,1,0:T(8,128)(2,1)S(1)}, u32[]{:S(2)}, u32[]{:S(2)}) collective-permute-start(bf16[2,64,512]{2,1,0:T(8,128)(2,1)S(1)} %get-tuple-element.36), channel_id=1, source_target_pairs={{0,2},{2,4},{4,6},{6,8},{8,10},{10,12},{12,14},{14,16},{16,18},{18... | collective-permute-start | bytes 393224 | tf_op jit(solution)/shard_map/ppermute | solution.py:20
  13.4 28.4 %collective-permute-start.1 = (bf16[2,64,512]{2,1,0:T(8,128)(2,1)S(1)}, bf16[2,64,512]{2,1,0:T(8,128)(2,1)}, u32[]{:S(2)}, u32[]{:S(2)}) collective-permute-start(bf16[2,64,512]{2,1,0:T(8,128)(2,1)S(1)} %get-tuple-element.37), channel_id=1, source_target_pairs={{2,0},{4,2},{6,4},{8,6},{10,8},{12,10},{14,12},{16,14},{18,16},{20... | collective-permute-start | bytes 393224 | tf_op jit(solution)/shard_map/ppermute | solution.py:22
  15.6 21.1 %copy-start.18 = (f32[2,64,512]{2,1,0:T(8,128)}, f32[2,64,512]{2,1,0:T(8,128)S(1)}, u32[]{:S(2)}) copy-start(f32[2,64,512]{2,1,0:T(8,128)S(1)} %collective-permute-done.2) | copy-start | bytes 786436
  15.9 24.2 %copy-start.9 = (bf16[128,512]{1,0:T(8,128)(2,1)S(1)}, bf16[128,512]{1,0:T(8,128)(2,1)}, u32[]{:S(2)}) copy-start(bf16[128,512]{1,0:T(8,128)(2,1)} %param.7) | copy-start | bytes 393220
  15.9 24.3 %copy-start.10 = (bf16[128,512]{1,0:T(8,128)(2,1)S(1)}, bf16[128,512]{1,0:T(8,128)(2,1)}, u32[]{:S(2)}) copy-start(bf16[128,512]{1,0:T(8,128)(2,1)} %param.6) | copy-start | bytes 393220
  16.0 12.1 %collective-permute-start.3 = (f32[2,64,512]{2,1,0:T(8,128)S(1)}, f32[2,64,512]{2,1,0:T(8,128)S(1)}, u32[]{:S(2)}, u32[]{:S(2)}) collective-permute-start(f32[2,64,512]{2,1,0:T(8,128)S(1)} %maximum_select_fusion), channel_id=1, source_target_pairs={{0,4},{2,6},{4,0},{6,2},{8,12},{10,14},{12,8},{14,10},{16,20},{18,... | collective-permute-start | bytes 786440 | tf_op jit(solution)/shard_map/ppermute | solution.py:32
  21.1 19.6 %copy-start.24 = (bf16[128,512]{1,0:T(8,128)(2,1)S(1)}, bf16[128,512]{1,0:T(8,128)(2,1)}, u32[]{:S(2)}) copy-start(bf16[128,512]{1,0:T(8,128)(2,1)} %param.5) | copy-start | bytes 393220
  28.1 11.9 %copy-start.20 = (f32[2,64,512]{2,1,0:T(8,128)}, f32[2,64,512]{2,1,0:T(8,128)S(1)}, u32[]{:S(2)}) copy-start(f32[2,64,512]{2,1,0:T(8,128)S(1)} %collective-permute-done.3) | copy-start | bytes 786436
  28.4 8.0 %collective-permute-start.4 = (f32[2,64,512]{2,1,0:T(8,128)S(1)}, f32[2,64,512]{2,1,0:T(8,128)S(1)}, u32[]{:S(2)}, u32[]{:S(2)}) collective-permute-start(f32[2,64,512]{2,1,0:T(8,128)S(1)} %maximum_select_fusion.1), channel_id=1, source_target_pairs={{0,8},{2,10},{4,12},{6,14},{8,0},{10,2},{12,4},{14,6},{16,24},{18,... | collective-permute-start | bytes 786440 | tf_op jit(solution)/shard_map/ppermute | solution.py:32
  37.4 8.2 %collective-permute-start.5 = (bf16[2,64,512]{2,1,0:T(8,128)(2,1)}, bf16[2,64,512]{2,1,0:T(8,128)(2,1)}, u32[]{:S(2)}, u32[]{:S(2)}) collective-permute-start(bf16[2,64,512]{2,1,0:T(8,128)(2,1)} %maximum_select_fusion.2), channel_id=1, source_target_pairs={{0,16},{2,18},{4,20},{6,22},{8,24},{10,26},{12,28},{14,30},{16,0},... | collective-permute-start | bytes 393224 | tf_op jit(solution)/shard_map/ppermute | solution.py:32
  41.3 11.8 %copy-start.11 = (bf16[2,64,8,64]{1,3,2,0:T(8,128)(2,1)}, bf16[2,64,8,64]{1,3,2,0:T(8,128)(2,1)S(1)}, u32[]{:S(2)}) copy-start(bf16[2,64,8,64]{1,3,2,0:T(8,128)(2,1)S(1)} %copy.107) | copy-start | bytes 393220
  44.8 8.4 %copy-start.13 = (bf16[2,64,8,64]{1,3,2,0:T(8,128)(2,1)}, bf16[2,64,8,64]{1,3,2,0:T(8,128)(2,1)S(1)}, u32[]{:S(2)}) copy-start(bf16[2,64,8,64]{1,3,2,0:T(8,128)(2,1)S(1)} %copy.108) | copy-start | bytes 393220
  45.2 8.0 %copy-start.15 = (bf16[2,64,8,64]{1,3,2,0:T(8,128)(2,1)}, bf16[2,64,8,64]{1,3,2,0:T(8,128)(2,1)S(1)}, u32[]{:S(2)}) copy-start(bf16[2,64,8,64]{1,3,2,0:T(8,128)(2,1)S(1)} %copy.106) | copy-start | bytes 393220
  74.0 4.6 %copy-start.8 = (f32[2,64,512]{1,2,0:T(8,128)S(1)}, f32[2,64,512]{1,2,0:T(8,128)}, u32[]{:S(2)}) copy-start(f32[2,64,512]{1,2,0:T(8,128)} %get-tuple-element.8) | copy-start | bytes 786436
  74.3 5.3 %copy-start.7 = (f32[2,64,512]{1,2,0:T(8,128)S(1)}, f32[2,64,512]{1,2,0:T(8,128)}, u32[]{:S(2)}) copy-start(f32[2,64,512]{1,2,0:T(8,128)} %get-tuple-element.12) | copy-start | bytes 786436
  75.4 5.1 %copy-start.6 = (f32[2,64,512]{1,2,0:T(8,128)S(1)}, f32[2,64,512]{1,2,0:T(8,128)}, u32[]{:S(2)}) copy-start(f32[2,64,512]{1,2,0:T(8,128)} %get-tuple-element.13) | copy-start | bytes 786436
  75.4 5.2 %copy-start.5 = (f32[2,64,512]{1,2,0:T(8,128)S(1)}, f32[2,64,512]{1,2,0:T(8,128)}, u32[]{:S(2)}) copy-start(f32[2,64,512]{1,2,0:T(8,128)} %get-tuple-element.11) | copy-start | bytes 786436
  80.8 7.9 %copy-start.3 = (f32[256,512]{0,1:T(8,128)S(1)}, f32[256,512]{0,1:T(8,128)}, u32[]{:S(2)}) copy-start(f32[256,512]{0,1:T(8,128)} %slice_reduce_fusion) | copy-start | bytes 1572868
  83.0 6.0 %copy-start.4 = (f32[256,512]{0,1:T(8,128)S(1)}, f32[256,512]{0,1:T(8,128)}, u32[]{:S(2)}) copy-start(f32[256,512]{0,1:T(8,128)} %slice_reduce_fusion.1) | copy-start | bytes 1572868
  83.8 36.4 %collective-permute-start.11 = (bf16[2,64,512]{2,1,0:T(8,128)(2,1)}, bf16[2,64,512]{2,1,0:T(8,128)(2,1)}, u32[]{:S(2)}, u32[]{:S(2)}) collective-permute-start(bf16[2,64,512]{2,1,0:T(8,128)(2,1)} %get-tuple-element.29), channel_id=1, source_target_pairs={{2,0},{4,2},{6,4},{8,6},{10,8},{12,10},{14,12},{16,14},{18,16},{20... | collective-permute-start | bytes 393224 | tf_op jit(solution)/shard_map/ppermute | solution.py:22
  85.1 35.2 %collective-permute-start.10 = (bf16[2,64,512]{2,1,0:T(8,128)(2,1)}, bf16[2,64,512]{2,1,0:T(8,128)(2,1)}, u32[]{:S(2)}, u32[]{:S(2)}) collective-permute-start(bf16[2,64,512]{2,1,0:T(8,128)(2,1)} %get-tuple-element.28), channel_id=1, source_target_pairs={{0,2},{2,4},{4,6},{6,8},{8,10},{10,12},{12,14},{14,16},{16,18},{18... | collective-permute-start | bytes 393224 | tf_op jit(solution)/shard_map/ppermute | solution.py:20
  89.2 9.8 %collective-permute-start.6 = (bf16[2,64,512]{2,1,0:T(8,128)(2,1)S(1)}, bf16[2,64,512]{2,1,0:T(8,128)(2,1)S(1)}, u32[]{:S(2)}, u32[]{:S(2)}) collective-permute-start(bf16[2,64,512]{2,1,0:T(8,128)(2,1)S(1)} %fusion.51), channel_id=1, source_target_pairs={{0,16},{2,18},{4,20},{6,22},{8,24},{10,26},{12,28},{14,30},{16,0},... | collective-permute-start | bytes 393224 | tf_op jit(solution)/shard_map/ppermute | solution.py:32
  99.3 5.6 %collective-permute-start.7 = (bf16[2,64,512]{2,1,0:T(8,128)(2,1)S(1)}, bf16[2,64,512]{2,1,0:T(8,128)(2,1)S(1)}, u32[]{:S(2)}, u32[]{:S(2)}) collective-permute-start(bf16[2,64,512]{2,1,0:T(8,128)(2,1)S(1)} %fusion.38), channel_id=1, source_target_pairs={{0,8},{2,10},{4,12},{6,14},{8,0},{10,2},{12,4},{14,6},{16,24},{18,... | collective-permute-start | bytes 393224 | tf_op jit(solution)/shard_map/ppermute | solution.py:32
  100.1 7.4 %copy-start.2 = (bf16[2,256,8,64]{1,3,2,0:T(8,128)(2,1)S(1)}, bf16[2,256,8,64]{1,3,2,0:T(8,128)(2,1)}, u32[]{:S(2)}) copy-start(bf16[2,256,8,64]{1,3,2,0:T(8,128)(2,1)} %copy-done.1) | copy-start | bytes 1572868
  100.1 7.4 %copy-start.12 = (bf16[2,64,8,64]{1,3,2,0:T(8,128)(2,1)S(1)}, bf16[2,64,8,64]{1,3,2,0:T(8,128)(2,1)}, u32[]{:S(2)}) copy-start(bf16[2,64,8,64]{1,3,2,0:T(8,128)(2,1)} %copy-done.11) | copy-start | bytes 393220
  100.1 7.4 %copy-start.14 = (bf16[2,64,8,64]{1,3,2,0:T(8,128)(2,1)S(1)}, bf16[2,64,8,64]{1,3,2,0:T(8,128)(2,1)}, u32[]{:S(2)}) copy-start(bf16[2,64,8,64]{1,3,2,0:T(8,128)(2,1)} %copy-done.13) | copy-start | bytes 393220
  106.0 15.9 %collective-permute-start.8 = (bf16[2,64,512]{2,1,0:T(8,128)(2,1)}, bf16[2,64,512]{2,1,0:T(8,128)(2,1)}, u32[]{:S(2)}, u32[]{:S(2)}) collective-permute-start(bf16[2,64,512]{2,1,0:T(8,128)(2,1)} %fusion.46), channel_id=1, source_target_pairs={{0,4},{2,6},{4,0},{6,2},{8,12},{10,14},{12,8},{14,10},{16,20},{18,... | collective-permute-start | bytes 393224 | tf_op jit(solution)/shard_map/ppermute | solution.py:32
  123.3 1.4 %collective-permute-start.9 = (bf16[2,64,512]{2,1,0:T(8,128)(2,1)S(1)}, bf16[2,64,512]{2,1,0:T(8,128)(2,1)S(1)}, u32[]{:S(2)}, u32[]{:S(2)}) collective-permute-start(bf16[2,64,512]{2,1,0:T(8,128)(2,1)S(1)} %fusion.42), channel_id=1, source_target_pairs={{0,2},{2,0},{4,6},{6,4},{8,10},{10,8},{12,14},{14,12},{16,18},{18,... | collective-permute-start | bytes 393224 | tf_op jit(solution)/shard_map/ppermute | solution.py:32
  (8 other events, 17.7 us)
Sparse Core Ops, SparseCore 0:
  75.5 15.8 reduce-scatter.1
where the time goes:
time: 137 us; the launch traced here: 136 us
  local copies, waits for them, and re-layouts  29.1 us (21%)
  matrix products  25.8 us (19%)
  waiting for transfers between devices  25.5 us (19%)
  starting transfers between devices  20.4 us (15%)
  other arithmetic  20.1 us (15%)
  between operations  14.9 us (11%)
    ppermute x8, waiting for transfers between devices, swapped(): return lax.ppermute(value, axis, pairs)  25.5 us
    dot_general x6, matrix products, score_product(): return jnp.einsum(form, left, right, preferred_element_type=jnp.float32)  24.2 us
    ppermute x8, starting transfers between devices, swapped(): return lax.ppermute(value, axis, pairs)  12.1 us
    ppermute x2, starting transfers between devices, with_halo(): lax.ppermute(tail, axis, [(i, (i + 1) % count) for i in range(ends)])  5.67 us
    convert_element_type x4, local copies, waits for them, and re-layouts, key_sets(): far_flat = far_source.astype(jnp.bfloat16).reshape(-1, feature_share)  4.56 us
    another operation x3, other arithmetic  4.56 us
    slice x4, local copies, waits for them, and re-layouts, return_scatter(): grad_sets[:, :block_length].reshape(row_share, feature_share)  3.8 us
    concatenate x12, local copies, waits for them, and re-layouts, key_sets(): return jnp.concatenate(target, axis=1)  3.17 us
  transfers between devices with their start and end apart: 13, of which 6 were waited for; matrix products, arithmetic and copies ran while one was open for 30% of the time, Pallas kernels for 0%

commit v1 on v0

v1 whole, which is shorter than its diff:
```python
import functools

import jax
import jax.numpy as jnp
from jax import lax
from jax.experimental import pallas as pl
from jax.experimental.pallas import tpu as pltpu
from jax.sharding import PartitionSpec as P

HEAD_DIM = 64
BLOCK = 64
ROWS = 128
PAIR = 2 * HEAD_DIM
HALO = 2 * BLOCK
FAR = HALO + ROWS
MESH = pl.DeviceIdType.MESH
BF16 = jnp.bfloat16
F32 = jnp.float32


def dot_nt(left, right):
    return lax.dot_general(
        left, right, (((1,), (1,)), ((), ())), preferred_element_type=F32
    )


def dot_nn(left, right):
    return jnp.dot(left, right, preferred_element_type=F32)


def each(count, step):
    if count <= 8:
        for i in range(count):
            step(i)
    else:
        lax.fori_loop(0, count, lambda i, c: (step(i), c)[1], 0)


def group_matrix(shape, token_dim, rows, first):
    group = ROWS // rows
    token = lax.broadcasted_iota(jnp.int32, shape, token_dim)
    other = lax.broadcasted_iota(jnp.int32, shape, 1 - token_dim)
    return jnp.where(token // group + first == other, 1.0 / group, 0.0).astype(BF16)


def kernel(n_seq, levels, *refs):
    q_in, k_in, v_in, w_in, dm_in, mixed_out, dq_out, dk_out, dv_out = refs[:9]
    (
        q, w, dm, kv, dattn, attn, dq, bias, gown, hsend, hrecv, gsend, grecv,
        mix_send, mix_recv, mix_own, dkv_stage, mixed_stage,
        in_sem, out_sem, halo_s, halo_r, far_s, far_r,
        ghalo_s, ghalo_r, gfar_s, gfar_r, mix_sem,
    ) = refs[9:38]
    rest = refs[38:]
    psend = rest[:levels]
    n_small = max(levels - 3, 0)
    srecv = rest[levels : levels + n_small]
    gssend = rest[levels + n_small : levels + 2 * n_small]
    gsrecv = rest[levels + 2 * n_small :]
    feats = q.shape[1]
    big = min(levels, 3)
    me = lax.axis_index("seq")
    hd = lax.axis_index("head")
    other_head = 1 - hd

    loads = [
        pltpu.make_async_copy(k_in, kv.at[0, HALO:FAR], in_sem.at[0]),
        pltpu.make_async_copy(v_in, kv.at[1, HALO:FAR], in_sem.at[1]),
        pltpu.make_async_copy(dm_in, dm, in_sem.at[2]),
        pltpu.make_async_copy(w_in, w, in_sem.at[3]),
        pltpu.make_async_copy(q_in, q, in_sem.at[4]),
    ]
    for load in loads:
        load.start()

    barrier = pltpu.get_barrier_semaphore()

    def greet(i):
        pl.semaphore_signal(
            barrier, 1, device_id={"seq": (me + 1 + i) % n_seq}, device_id_type=MESH
        )

    lax.fori_loop(0, n_seq - 1, lambda i, c: (greet(i), c)[1], 0)
    pl.semaphore_signal(barrier, 1, device_id={"head": other_head}, device_id_type=MESH)

    @pl.when(me == 0)
    def _():
        kv[:, 0:BLOCK, :] = jnp.zeros((2, BLOCK, feats), BF16)
        hrecv[:, 0:BLOCK, :] = jnp.zeros((2, BLOCK, feats), BF16)

    @pl.when(me == n_seq - 1)
    def _():
        kv[:, BLOCK:HALO, :] = jnp.zeros((2, BLOCK, feats), BF16)
        hrecv[:, BLOCK:HALO, :] = jnp.zeros((2, BLOCK, feats), BF16)

    second = (lax.broadcasted_iota(jnp.int32, (8, 2 * ROWS), 1) // BLOCK) % 2
    missing = ((second == 0) & (me == 0)) | ((second == 1) & (me == n_seq - 1))
    bias[...] = jnp.where(missing, -jnp.inf, 0.0)

    loads[0].wait()
    loads[1].wait()

    spans = []
    for b in range(levels):
        size = 2**b
        span = me // size
        sibling = (span + 1 - 2 * (span % 2)) * size
        mine = me % size
        spans.append((size, BLOCK >> b, sibling, mine))

    k_own = kv[0, HALO:FAR, :]
    v_own = kv[1, HALO:FAR, :]
    for b, (size, rows, sibling, mine) in enumerate(spans):
        if b < 3:
            mat = group_matrix((rows, ROWS), 1, rows, 0)
            psend[b][0] = dot_nn(mat, k_own).astype(BF16)
            psend[b][1] = dot_nn(mat, v_own).astype(BF16)
        else:
            mat = group_matrix((8, ROWS), 1, rows, (mine * rows) % 8)
            psend[b][...] = jnp.concatenate(
                [dot_nn(mat, k_own), dot_nn(mat, v_own)], axis=0
            ).astype(BF16)

    pl.semaphore_wait(barrier, n_seq)

    def halo_copy(way):
        if way == 0:
            src, dst, to = kv.at[:, HALO + BLOCK : FAR], kv.at[:, 0:BLOCK], me + 1
        else:
            src, dst, to = kv.at[:, HALO : HALO + BLOCK], kv.at[:, BLOCK:HALO], me - 1
        return pltpu.make_async_remote_copy(
            src, dst, halo_s.at[way], halo_r.at[way],
            device_id={"seq": to}, device_id_type=MESH,
        )

    def far_copy(b, dest, slot):
        size, rows, sibling, mine = spans[b]
        if b < 3:
            dst = kv.at[:, pl.ds(pl.multiple_of(FAR + BLOCK * b + slot * rows, 16), rows)]
        else:
            dst = srecv[b - 3].at[slot]
        return pltpu.make_async_remote_copy(
            psend[b], dst, far_s.at[size - 1 + dest], far_r.at[size - 1 + slot],
            device_id={"seq": sibling + dest}, device_id_type=MESH,
        )

    for b in reversed(range(levels)):
        each(2**b, lambda i, b=b: far_copy(b, i, spans[b][3]).start())

    has_next = me < n_seq - 1
    has_prev = me > 0
    pl.when(has_next)(lambda: halo_copy(0).start())
    pl.when(has_prev)(lambda: halo_copy(1).start())

    loads[2].wait()
    loads[3].wait()
    dattn[...] = dot_nt(dm[...], w[...]).astype(BF16)
    loads[4].wait()

    pl.when(has_prev)(lambda: halo_copy(0).wait_recv())
    pl.when(has_next)(lambda: halo_copy(1).wait_recv())
    for b in range(levels):
        each(2**b, lambda i, b=b: far_copy(b, 0, i).wait_recv())

    for b in range(3, levels):
        rows = spans[b][1]
        per = 8 // rows
        pieces = []
        for g in range(8):
            total = srecv[b - 3][g * per].astype(F32)
            for s in range(1, per):
                total = total + srecv[b - 3][g * per + s].astype(F32)
            pieces.append(total)
        at = FAR + BLOCK * b
        for part in range(2):
            kv[part, at : at + BLOCK, :] = jnp.concatenate(
                [piece[8 * part : 8 * part + 8] for piece in pieces], axis=0
            ).astype(BF16)

    lane = lax.broadcasted_iota(jnp.int32, (1, PAIR), 1)
    head_a = jnp.where(lane < HEAD_DIM, 1.0, 0.0).astype(BF16)
    head_b = jnp.where(lane < HEAD_DIM, 0.0, 1.0).astype(BF16)
    token = (lax.broadcasted_iota(jnp.int32, (1, 2 * ROWS), 1) // BLOCK) % 2
    first = token == 0
    mask0 = jnp.where(first, 1.0, 0.0)
    mask1 = jnp.where(first, 0.0, 1.0)

    for pair in range(feats // PAIR):
        cols = slice(pair * PAIR, (pair + 1) * PAIR)
        qp = q[:, cols] * jnp.asarray(0.125, BF16)
        dap = dattn[:, cols]
        qs = jnp.concatenate([qp * head_a, qp * head_b], axis=0)
        das = jnp.concatenate([dap * head_a, dap * head_b], axis=0)
        kp = kv[0, :, cols]
        vp = kv[1, :, cols]

        def merge(full):
            halo = jnp.where(first, full[:BLOCK], full[BLOCK:HALO])
            return halo, full[HALO:]

        s_halo, s_rest = merge(dot_nt(kp, qs))
        s_all = jnp.concatenate([s_halo + bias[0:1, :], s_rest], axis=0)
        top = jnp.max(s_all, axis=0, keepdims=True)
        e_all = jnp.exp(s_all - top)
        normed = e_all * (1.0 / jnp.sum(e_all, axis=0, keepdims=True))

        def unmerge(full):
            halo = full[:BLOCK]
            return jnp.concatenate(
                [halo * mask0, halo * mask1, full[BLOCK:]], axis=0
            ).astype(BF16)

        weights = unmerge(normed)
        d_halo, d_rest = merge(dot_nt(vp, das))
        d_normed = jnp.concatenate([d_halo, d_rest], axis=0)
        inner = jnp.sum(normed * d_normed, axis=0, keepdims=True)
        d_scores = unmerge(normed * (d_normed - inner))

        def both(values_t, coeffs):
            full = dot_nn(values_t, coeffs)
            return jnp.concatenate(
                [full[:HEAD_DIM, :ROWS], full[HEAD_DIM:, ROWS:]], axis=0
            ).T

        attn[:, cols] = both(vp.T, weights).astype(BF16)
        dq[:, cols] = (both(kp.T, d_scores) * 0.125).astype(BF16)
        grads = (dot_nn(d_scores, qs), dot_nn(weights, das))
        for part in range(2):
            grad = grads[part]
            hsend[part, :, cols] = grad[:HALO].astype(BF16)
            gown[part, :, cols] = grad[HALO:FAR]
            gsend[part, :, cols] = grad[FAR : FAR + BLOCK * big].astype(BF16)
        for b in range(3, levels):
            at = FAR + BLOCK * b
            for g in range(8):
                gssend[b - 3][g, :, cols] = jnp.concatenate(
                    [grad[at + 8 * g : at + 8 * g + 8] for grad in grads], axis=0
                ).astype(BF16)

    def ghalo_copy(way):
        if way == 0:
            src, dst, to = hsend.at[:, 0:BLOCK], hrecv.at[:, BLOCK:HALO], me - 1
        else:
            src, dst, to = hsend.at[:, BLOCK:HALO], hrecv.at[:, 0:BLOCK], me + 1
        return pltpu.make_async_remote_copy(
            src, dst, ghalo_s.at[way], ghalo_r.at[way],
            device_id={"seq": to}, device_id_type=MESH,
        )

    def gfar_copy(b, dest, slot):
        size, rows, sibling, mine = spans[b]
        if b < 3:
            src = gsend.at[:, pl.ds(pl.multiple_of(BLOCK * b + dest * rows, 16), rows)]
            dst = grecv.at[:, pl.ds(pl.multiple_of(BLOCK * b + slot * rows, 16), rows)]
        else:
            src = gssend[b - 3].at[dest // (8 // rows)]
            dst = gsrecv[b - 3].at[slot]
        return pltpu.make_async_remote_copy(
            src, dst, gfar_s.at[size - 1 + dest], gfar_r.at[size - 1 + slot],
            device_id={"seq": sibling + dest}, device_id_type=MESH,
        )

    for b in reversed(range(levels)):
        each(2**b, lambda i, b=b: gfar_copy(b, i, spans[b][3]).start())
    pl.when(has_prev)(lambda: ghalo_copy(0).start())
    pl.when(has_next)(lambda: ghalo_copy(1).start())

    dq_store = pltpu.make_async_copy(dq, dq_out, out_sem.at[0])
    dq_store.start()

    theirs = pl.ds(pl.multiple_of(other_head * BLOCK, BLOCK), BLOCK)
    ours = pl.ds(pl.multiple_of(hd * BLOCK, BLOCK), BLOCK)
    mix_send[...] = dot_nn(attn[theirs, :], w[...]).astype(BF16)
    mix_copy = pltpu.make_async_remote_copy(
        mix_send, mix_recv, mix_sem.at[0], mix_sem.at[1],
        device_id={"head": other_head}, device_id_type=MESH,
    )
    mix_copy.start()
    mix_own[...] = dot_nn(attn[ours, :], w[...])

    pl.when(has_next)(lambda: ghalo_copy(0).wait_recv())
    pl.when(has_prev)(lambda: ghalo_copy(1).wait_recv())
    for b in range(levels):
        each(2**b, lambda i, b=b: gfar_copy(b, 0, i).wait_recv())

    stores = []
    for part in range(2):
        total = gown[part] + hrecv[part].astype(F32)
        for b, (size, rows, sibling, mine) in enumerate(spans):
            if b < 3:
                token = lax.broadcasted_iota(jnp.int32, (ROWS, BLOCK), 0)
                row = lax.broadcasted_iota(jnp.int32, (ROWS, BLOCK), 1)
                group = ROWS // rows
                mat = jnp.where(token // group == row % rows, 1.0 / group, 0.0).astype(BF16)
                total = total + dot_nn(mat, grecv[part, BLOCK * b : BLOCK * (b + 1), :])
            else:
                wide = 16 * size
                token = lax.broadcasted_iota(jnp.int32, (ROWS, wide), 0)
                row = lax.broadcasted_iota(jnp.int32, (ROWS, wide), 1) % 16
                group = ROWS // rows
                wanted = token // group + (mine * rows) % 8 + 8 * part
                mat = jnp.where(wanted == row, 1.0 / group, 0.0).astype(BF16)
                total = total + dot_nn(mat, gsrecv[b - 3][...].reshape(wide, feats))
        dkv_stage[part] = total.astype(BF16)
        store = pltpu.make_async_copy(
            dkv_stage.at[part], (dk_out, dv_out)[part], out_sem.at[1 + part]
        )
        store.start()
        stores.append(store)

    mix_copy.wait_recv()
    mixed_stage[...] = (mix_own[...] + mix_recv[...].astype(F32)).astype(BF16)
    mixed_store = pltpu.make_async_copy(mixed_stage, mixed_out, out_sem.at[3])
    mixed_store.start()

    pl.when(has_next)(lambda: halo_copy(0).wait_send())
    pl.when(has_prev)(lambda: halo_copy(1).wait_send())
    pl.when(has_prev)(lambda: ghalo_copy(0).wait_send())
    pl.when(has_next)(lambda: ghalo_copy(1).wait_send())
    for b in range(levels):
        each(2**b, lambda i, b=b: far_copy(b, i, spans[b][3]).wait_send())
        each(2**b, lambda i, b=b: gfar_copy(b, i, spans[b][3]).wait_send())
    mix_copy.wait_send()
    dq_store.wait()
    for store in stores:
        store.wait()
    mixed_store.wait()


def on_device(n_seq, queries, keys, values, w_out, d_mixed):
    feats = queries.shape[1]
    width = w_out.shape[1]
    levels = n_seq.bit_length() - 1
    big = min(levels, 3)
    small = list(range(3, levels))
    n_keys = FAR + BLOCK * levels
    vmem = pltpu.VMEM
    dma = pltpu.SemaphoreType.DMA
    scratch = [
        vmem((ROWS, feats), BF16),
        vmem((feats, width), BF16),
        vmem((ROWS, width), BF16),
        vmem((2, n_keys, feats), BF16),
        vmem((ROWS, feats), BF16),
        vmem((ROWS, feats), BF16),
        vmem((ROWS, feats), BF16),
        vmem((8, 2 * ROWS), F32),
        vmem((2, ROWS, feats), F32),
        vmem((2, HALO, feats), BF16),
        vmem((2, HALO, feats), BF16),
        vmem((2, BLOCK * big, feats), BF16),
        vmem((2, BLOCK * big, feats), BF16),
        vmem((BLOCK, width), BF16),
        vmem((BLOCK, width), BF16),
        vmem((BLOCK, width), F32),
        vmem((2, ROWS, feats), BF16),
        vmem((BLOCK, width), BF16),
        dma((5,)),
        dma((4,)),
        dma((2,)),
        dma((2,)),
        dma((n_seq - 1,)),
        dma((n_seq - 1,)),
        dma((2,)),
        dma((2,)),
        dma((n_seq - 1,)),
        dma((n_seq - 1,)),
        dma((2,)),
    ]
    scratch += [vmem((2, BLOCK >> b, feats), BF16) for b in range(big)]
    scratch += [vmem((16, feats), BF16) for b in small]
    scratch += [vmem((2**b, 16, feats), BF16) for b in small]
    scratch += [vmem((8, 16, feats), BF16) for b in small]
    scratch += [vmem((2**b, 16, feats), BF16) for b in small]
    anywhere = pl.BlockSpec(memory_space=pl.ANY)
    return pl.pallas_call(
        functools.partial(kernel, n_seq, levels),
        out_shape=[
            jax.ShapeDtypeStruct((BLOCK, width), BF16),
            jax.ShapeDtypeStruct((ROWS, feats), BF16),
            jax.ShapeDtypeStruct((ROWS, feats), BF16),
            jax.ShapeDtypeStruct((ROWS, feats), BF16),
        ],
        in_specs=[anywhere] * 5,
        out_specs=[anywhere] * 4,
        scratch_shapes=scratch,
        compiler_params=pltpu.CompilerParams(
            collective_id=0, has_side_effects=True, vmem_limit_bytes=40 * 2**20
        ),
    )(queries, keys, values, w_out, d_mixed)


def solution(mesh):
    in_specs = (
        P("seq", "head"),
        P("seq", "head"),
        P("seq", "head"),
        P("head", None),
        P("seq", None),
    )
    out_specs = (P(("seq", "head"), None), P("seq", "head"), P("seq", "head"), P("seq", "head"))
    return jax.shard_map(
        functools.partial(on_device, mesh.shape["seq"]),
        mesh=mesh,
        in_specs=in_specs,
        out_specs=out_specs,
        check_vma=False,
    )
```

time: 137 us -> 38 us (0.28)
  the two profiles are of different devices: /device:TPU:0 before, /device:TPU:13 now
where the time goes in v1:
time: 38 us; the launch traced here: 37.7 us
  Pallas kernels  29.6 us (78%)
  local copies, waits for them, and re-layouts  7.5 us (20%)
  between operations  0.65 us (2%)
    pallas_call x1, Pallas kernels, on_device(): pl.pallas_call(functools.partial(kernel, n_seq, levels), out_shape=[jax.S...  29.6 us
    unnamed x14, local copies, waits for them, and re-layouts  7.5 us

profile of v1, /device:TPU:13, one launch (start us, length us, event | category | flops | bytes accessed | tf_op | source)
XLA Modules:
  0.0 37.7 jit_solution(3441554532232683095)
XLA Ops:
  0.6 0.0 copy-start
  0.6 1.2 %copy-done = bf16[512,1024]{1,0:T(8,128)(2,1)S(1)} copy-done((bf16[512,1024]{1,0:T(8,128)(2,1)S(1)}, bf16[512,1024]{1,0:T(8,128)(2,1)}, u32[]{:S(2)}) %copy-start) | copy-done | bytes 1048600
  1.9 0.0 copy-start.1
  1.9 0.9 %copy-done.1 = bf16[128,1024]{1,0:T(8,128)(2,1)S(1)} copy-done((bf16[128,1024]{1,0:T(8,128)(2,1)S(1)}, bf16[128,1024]{1,0:T(8,128)(2,1)}, u32[]{:S(2)}) %copy-start.1) | copy-done | bytes 262168
  2.8 0.0 copy-start.2
  2.8 0.9 %copy-done.2 = bf16[128,512]{1,0:T(8,128)(2,1)S(1)} copy-done((bf16[128,512]{1,0:T(8,128)(2,1)S(1)}, bf16[128,512]{1,0:T(8,128)(2,1)}, u32[]{:S(2)}) %copy-start.2) | copy-done | bytes 131096
  3.7 0.0 copy-start.3
  3.7 0.9 %copy-done.3 = bf16[128,512]{1,0:T(8,128)(2,1)S(1)} copy-done((bf16[128,512]{1,0:T(8,128)(2,1)S(1)}, bf16[128,512]{1,0:T(8,128)(2,1)}, u32[]{:S(2)}) %copy-start.3) | copy-done | bytes 131096
  4.6 0.0 copy-start.4
  4.6 0.9 %copy-done.4 = bf16[128,512]{1,0:T(8,128)(2,1)S(1)} copy-done((bf16[128,512]{1,0:T(8,128)(2,1)S(1)}, bf16[128,512]{1,0:T(8,128)(2,1)}, u32[]{:S(2)}) %copy-start.4) | copy-done | bytes 131096
  5.5 29.6 %shard_map.84 = (bf16[64,1024]{1,0:T(8,128)(2,1)S(1)}, bf16[128,512]{1,0:T(8,128)(2,1)S(1)}, bf16[128,512]{1,0:T(8,128)(2,1)S(1)}, bf16[128,512]{1,0:T(8,128)(2,1)S(1)}) custom-call(bf16[128,512]{1,0:T(8,128)(2,1)S(1)} %copy-done.2, bf16[128,512]{1,0:T(8,128)(2,1)S(1)} %copy-done.3, bf16[128,512]{1,0:T(8,128)(2,1)S(1)} %copy-done.4, ...), custom_call_target="tpu_custom_call" | custom-call | tf_op jit(solution)/shard_map/pallas_call | solution.py:376
  35.1 0.7 %copy.13 = bf16[64,1024]{1,0:T(8,128)(2,1)} copy(bf16[64,1024]{1,0:T(8,128)(2,1)S(1)} %get-tuple-element.8) | data formatting | bytes 262144
  35.8 0.7 %copy.14 = bf16[128,512]{1,0:T(8,128)(2,1)} copy(bf16[128,512]{1,0:T(8,128)(2,1)S(1)} %get-tuple-element.9) | data formatting | bytes 262144
  36.4 0.7 %copy.15 = bf16[128,512]{1,0:T(8,128)(2,1)} copy(bf16[128,512]{1,0:T(8,128)(2,1)S(1)} %get-tuple-element.10) | data formatting | bytes 262144
  37.1 0.7 %copy.16 = bf16[128,512]{1,0:T(8,128)(2,1)} copy(bf16[128,512]{1,0:T(8,128)(2,1)S(1)} %get-tuple-element.11) | data formatting | bytes 262144
Async XLA Ops:
  0.6 1.2 %copy-start = (bf16[512,1024]{1,0:T(8,128)(2,1)S(1)}, bf16[512,1024]{1,0:T(8,128)(2,1)}, u32[]{:S(2)}) copy-start(bf16[512,1024]{1,0:T(8,128)(2,1)} %refs_3_.1) | copy-start | bytes 3145732
  1.9 0.9 %copy-start.1 = (bf16[128,1024]{1,0:T(8,128)(2,1)S(1)}, bf16[128,1024]{1,0:T(8,128)(2,1)}, u32[]{:S(2)}) copy-start(bf16[128,1024]{1,0:T(8,128)(2,1)} %refs_4_.1) | copy-start | bytes 786436
  2.8 0.9 %copy-start.2 = (bf16[128,512]{1,0:T(8,128)(2,1)S(1)}, bf16[128,512]{1,0:T(8,128)(2,1)}, u32[]{:S(2)}) copy-start(bf16[128,512]{1,0:T(8,128)(2,1)} %refs_0_.1) | copy-start | bytes 393220
  3.7 0.9 %copy-start.3 = (bf16[128,512]{1,0:T(8,128)(2,1)S(1)}, bf16[128,512]{1,0:T(8,128)(2,1)}, u32[]{:S(2)}) copy-start(bf16[128,512]{1,0:T(8,128)(2,1)} %refs_1_.1) | copy-start | bytes 393220
  4.6 0.9 %copy-start.4 = (bf16[128,512]{1,0:T(8,128)(2,1)S(1)}, bf16[128,512]{1,0:T(8,128)(2,1)}, u32[]{:S(2)}) copy-start(bf16[128,512]{1,0:T(8,128)(2,1)} %refs_2_.1) | copy-start | bytes 393220

commit v2 on v1

--- a/solution.py
+++ b/solution.py
@@ -44,14 +44,15 @@
 
 
 def kernel(n_seq, levels, *refs):
-    q_in, k_in, v_in, w_in, dm_in, mixed_out, dq_out, dk_out, dv_out = refs[:9]
+    q_in, k_in, v_in, w_in, dm_in, mixed_out, dq, dk_out, dv_out = refs[:9]
     (
-        q, w, dm, kv, dattn, attn, dq, bias, gown, hsend, hrecv, gsend, grecv,
-        mix_send, mix_recv, mix_own, dkv_stage, mixed_stage,
-        in_sem, out_sem, halo_s, halo_r, far_s, far_r,
+        q, w, dm, kv, dattn, attn, bias, gown, hsend, hrecv, gsend, grecv,
+        mix_send, mix_recv, mix_own,
+        in_sem, halo_s, halo_r, far_s, far_r,
         ghalo_s, ghalo_r, gfar_s, gfar_r, mix_sem,
-    ) = refs[9:38]
-    rest = refs[38:]
+        relay_s, relay_r, sum_s, sum_r, sum_recv, sum_send, small_recv, small_send,
+    ) = refs[9:42]
+    rest = refs[42:]
     psend = rest[:levels]
     n_small = max(levels - 3, 0)
     srecv = rest[levels : levels + n_small]
@@ -62,6 +63,8 @@
     me = lax.axis_index("seq")
     hd = lax.axis_index("head")
     other_head = 1 - hd
+    core = me % 2
+    twin = me + 1 - 2 * core
 
     loads = [
         pltpu.make_async_copy(k_in, kv.at[0, HALO:FAR], in_sem.at[0]),
@@ -75,12 +78,17 @@
 
     barrier = pltpu.get_barrier_semaphore()
 
-    def greet(i):
-        pl.semaphore_signal(
-            barrier, 1, device_id={"seq": (me + 1 + i) % n_seq}, device_id_type=MESH
-        )
-
-    lax.fori_loop(0, n_seq - 1, lambda i, c: (greet(i), c)[1], 0)
+    def greet(place):
+        pl.semaphore_signal(barrier, 1, device_id={"seq": place}, device_id_type=MESH)
+
+    across = me - 1 + 2 * core
+    has_across = (me > 0) & (me < n_seq - 1)
+    if levels > 4:
+        each(n_seq - 1, lambda i: greet((me + 1 + i) % n_seq))
+    else:
+        each(n_seq // 2 - 1, lambda i: greet((me + 2 + 2 * i) % n_seq))
+        greet(twin)
+        pl.when(has_across)(lambda: greet(across))
     pl.semaphore_signal(barrier, 1, device_id={"head": other_head}, device_id_type=MESH)
 
     @pl.when(me == 0)
@@ -121,7 +129,12 @@
                 [dot_nn(mat, k_own), dot_nn(mat, v_own)], axis=0
             ).astype(BF16)
 
-    pl.semaphore_wait(barrier, n_seq)
+    if levels > 4:
+        pl.semaphore_wait(barrier, n_seq)
+    else:
+        greeted = n_seq // 2 + 1
+        pl.when(has_across)(lambda: pl.semaphore_wait(barrier, greeted + 1))
+        pl.when(jnp.logical_not(has_across))(lambda: pl.semaphore_wait(barrier, greeted))
 
     def halo_copy(way):
         if way == 0:
@@ -133,19 +146,43 @@
             device_id={"seq": to}, device_id_type=MESH,
         )
 
+    relayed = list(range(1, min(levels, 4)))
+
+    def count(b):
+        return 2 ** (b - 1) if b in relayed else 2**b
+
+    def key_rows(b, at, n):
+        return kv.at[:, pl.ds(pl.multiple_of(FAR + BLOCK * b + at, 16), n)]
+
     def far_copy(b, dest, slot):
         size, rows, sibling, mine = spans[b]
+        to = sibling + dest
+        if b in relayed:
+            slot = core * (size // 2) + slot
+            to = sibling + 2 * dest + core
+        dst = key_rows(b, slot * rows, rows) if b < 3 else srecv[b - 3].at[slot]
+        return pltpu.make_async_remote_copy(
+            psend[b], dst, far_s.at[size - 1 + dest], far_r.at[size - 1 + slot],
+            device_id={"seq": to}, device_id_type=MESH,
+        )
+
+    def my_slot(b):
+        return mine_of[b] // 2 if b in relayed else mine_of[b]
+
+    mine_of = [span[3] for span in spans]
+
+    def relay_copy(b, part):
         if b < 3:
-            dst = kv.at[:, pl.ds(pl.multiple_of(FAR + BLOCK * b + slot * rows, 16), rows)]
-        else:
-            dst = srecv[b - 3].at[slot]
-        return pltpu.make_async_remote_copy(
-            psend[b], dst, far_s.at[size - 1 + dest], far_r.at[size - 1 + slot],
-            device_id={"seq": sibling + dest}, device_id_type=MESH,
+            ref = key_rows(b, part * (BLOCK // 2), BLOCK // 2)
+        else:
+            ref = srecv[0].at[pl.ds(part * 4, 4)]
+        return pltpu.make_async_remote_copy(
+            ref, ref, relay_s.at[b], relay_r.at[b],
+            device_id={"seq": twin}, device_id_type=MESH,
         )
 
     for b in reversed(range(levels)):
-        each(2**b, lambda i, b=b: far_copy(b, i, spans[b][3]).start())
+        each(count(b), lambda i, b=b: far_copy(b, i, my_slot(b)).start())
 
     has_next = me < n_seq - 1
     has_prev = me > 0
@@ -160,14 +197,21 @@
     pl.when(has_prev)(lambda: halo_copy(0).wait_recv())
     pl.when(has_next)(lambda: halo_copy(1).wait_recv())
     for b in range(levels):
-        each(2**b, lambda i, b=b: far_copy(b, 0, i).wait_recv())
+        each(count(b), lambda i, b=b: far_copy(b, 0, i).wait_recv())
+        if b in relayed:
+            relay_copy(b, core).start()
+    for b in relayed:
+        relay_copy(b, 1 - core).wait_recv()
+
+    def place(b, slot):
+        return (slot % 2) * 4 + slot // 2 if b == 3 else slot
 
     for b in range(3, levels):
         rows = spans[b][1]
         per = 8 // rows
         pieces = []
         for g in range(8):
-            total = srecv[b - 3][g * per].astype(F32)
+            total = srecv[b - 3][place(b, g * per)].astype(F32)
             for s in range(1, per):
                 total = total + srecv[b - 3][g * per + s].astype(F32)
             pieces.append(total)
@@ -233,7 +277,7 @@
         for b in range(3, levels):
             at = FAR + BLOCK * b
             for g in range(8):
-                gssend[b - 3][g, :, cols] = jnp.concatenate(
+                gssend[b - 3][place(b, g), :, cols] = jnp.concatenate(
                     [grad[at + 8 * g : at + 8 * g + 8] for grad in grads], axis=0
                 ).astype(BF16)
 
@@ -247,26 +291,58 @@
             device_id={"seq": to}, device_id_type=MESH,
         )
 
+    def sum_copy(b):
+        half = BLOCK // 2
+        if b < 3:
+            at = BLOCK * b + (1 - core) * half
+            src = gsend.at[:, pl.ds(pl.multiple_of(at, half), half)]
+            dst = sum_recv.at[:, half * (b - 1) : half * b]
+        else:
+            src = gssend[0].at[pl.ds((1 - core) * 4, 4)]
+            dst = small_recv
+        return pltpu.make_async_remote_copy(
+            src, dst, sum_s.at[b], sum_r.at[b],
+            device_id={"seq": twin}, device_id_type=MESH,
+        )
+
     def gfar_copy(b, dest, slot):
         size, rows, sibling, mine = spans[b]
-        if b < 3:
-            src = gsend.at[:, pl.ds(pl.multiple_of(BLOCK * b + dest * rows, 16), rows)]
-            dst = grecv.at[:, pl.ds(pl.multiple_of(BLOCK * b + slot * rows, 16), rows)]
+        to = sibling + dest
+        if b == 0:
+            src, dst = gsend.at[:, 0:BLOCK], grecv.at[:, 0:BLOCK]
+        elif b < 3:
+            half = BLOCK // 2
+            src = sum_send.at[:, pl.ds(pl.multiple_of(half * (b - 1) + dest * rows, 16), rows)]
+            dst = grecv.at[:, pl.ds(pl.multiple_of(half * (b + 1) + slot * rows, 16), rows)]
+        elif b == 3:
+            src, dst = small_send.at[dest], gsrecv[0].at[slot]
         else:
             src = gssend[b - 3].at[dest // (8 // rows)]
             dst = gsrecv[b - 3].at[slot]
+        if b in relayed:
+            to = sibling + 2 * dest + core
         return pltpu.make_async_remote_copy(
             src, dst, gfar_s.at[size - 1 + dest], gfar_r.at[size - 1 + slot],
-            device_id={"seq": sibling + dest}, device_id_type=MESH,
-        )
-
-    for b in reversed(range(levels)):
-        each(2**b, lambda i, b=b: gfar_copy(b, i, spans[b][3]).start())
+            device_id={"seq": to}, device_id_type=MESH,
+        )
+
+    for b in reversed(relayed):
+        sum_copy(b).start()
     pl.when(has_prev)(lambda: ghalo_copy(0).start())
     pl.when(has_next)(lambda: ghalo_copy(1).start())
-
-    dq_store = pltpu.make_async_copy(dq, dq_out, out_sem.at[0])
-    dq_store.start()
+    for b in reversed(range(levels)):
+        if b in relayed:
+            sum_copy(b).wait_recv()
+            half = BLOCK // 2
+            if b < 3:
+                mine_rows = pl.ds(pl.multiple_of(BLOCK * b + core * half, half), half)
+                own = gsend[:, mine_rows, :].astype(F32)
+                both_cores = own + sum_recv[:, half * (b - 1) : half * b, :].astype(F32)
+                sum_send[:, half * (b - 1) : half * b, :] = both_cores.astype(BF16)
+            else:
+                own = gssend[0][pl.ds(core * 4, 4)].astype(F32)
+                small_send[...] = (own + small_recv[...].astype(F32)).astype(BF16)
+        each(count(b), lambda i, b=b: gfar_copy(b, i, my_slot(b)).start())
 
     theirs = pl.ds(pl.multiple_of(other_head * BLOCK, BLOCK), BLOCK)
     ours = pl.ds(pl.multiple_of(hd * BLOCK, BLOCK), BLOCK)
@@ -281,50 +357,48 @@
     pl.when(has_next)(lambda: ghalo_copy(0).wait_recv())
     pl.when(has_prev)(lambda: ghalo_copy(1).wait_recv())
     for b in range(levels):
-        each(2**b, lambda i, b=b: gfar_copy(b, 0, i).wait_recv())
-
-    stores = []
+        each(count(b), lambda i, b=b: gfar_copy(b, 0, i).wait_recv())
+
     for part in range(2):
         total = gown[part] + hrecv[part].astype(F32)
         for b, (size, rows, sibling, mine) in enumerate(spans):
             if b < 3:
-                token = lax.broadcasted_iota(jnp.int32, (ROWS, BLOCK), 0)
-                row = lax.broadcasted_iota(jnp.int32, (ROWS, BLOCK), 1)
+                wide = rows * count(b)
+                at = BLOCK // 2 * (b + 1) if b else 0
+                token = lax.broadcasted_iota(jnp.int32, (ROWS, wide), 0)
+                row = lax.broadcasted_iota(jnp.int32, (ROWS, wide), 1)
                 group = ROWS // rows
                 mat = jnp.where(token // group == row % rows, 1.0 / group, 0.0).astype(BF16)
-                total = total + dot_nn(mat, grecv[part, BLOCK * b : BLOCK * (b + 1), :])
+                total = total + dot_nn(mat, grecv[part, at : at + wide, :])
             else:
-                wide = 16 * size
+                wide = 16 * count(b)
                 token = lax.broadcasted_iota(jnp.int32, (ROWS, wide), 0)
                 row = lax.broadcasted_iota(jnp.int32, (ROWS, wide), 1) % 16
                 group = ROWS // rows
                 wanted = token // group + (mine * rows) % 8 + 8 * part
                 mat = jnp.where(wanted == row, 1.0 / group, 0.0).astype(BF16)
                 total = total + dot_nn(mat, gsrecv[b - 3][...].reshape(wide, feats))
-        dkv_stage[part] = total.astype(BF16)
-        store = pltpu.make_async_copy(
-            dkv_stage.at[part], (dk_out, dv_out)[part], out_sem.at[1 + part]
-        )
-        store.start()
-        stores.append(store)
+        (dk_out, dv_out)[part][...] = total.astype(BF16)
 
     mix_copy.wait_recv()
-    mixed_stage[...] = (mix_own[...] + mix_recv[...].astype(F32)).astype(BF16)
-    mixed_store = pltpu.make_async_copy(mixed_stage, mixed_out, out_sem.at[3])
-    mixed_store.start()
+    mixed_out[...] = (mix_own[...] + mix_recv[...].astype(F32)).astype(BF16)
 
     pl.when(has_next)(lambda: halo_copy(0).wait_send())
     pl.when(has_prev)(lambda: halo_copy(1).wait_send())
     pl.when(has_prev)(lambda: ghalo_copy(0).wait_send())
     pl.when(has_next)(lambda: ghalo_copy(1).wait_send())
     for b in range(levels):
-        each(2**b, lambda i, b=b: far_copy(b, i, spans[b][3]).wait_send())
-        each(2**b, lambda i, b=b: gfar_copy(b, i, spans[b][3]).wait_send())
+        each(count(b), lambda i, b=b: far_copy(b, i, my_slot(b)).wait_send())
+        each(count(b), lambda i, b=b: gfar_copy(b, i, my_slot(b)).wait_send())
+    for b in relayed:
+        relay_copy(b, core).wait_send()
+        sum_copy(b).wait_send()
     mix_copy.wait_send()
-    dq_store.wait()
-    for store in stores:
-        store.wait()
-    mixed_store.wait()
+
+
+def write_kernel(*refs):
+    for i in range(4):
+        refs[4 + i][...] = refs[i][...]
 
 
 def on_device(n_seq, queries, keys, values, w_out, d_mixed):
@@ -343,20 +417,16 @@
         vmem((2, n_keys, feats), BF16),
         vmem((ROWS, feats), BF16),
         vmem((ROWS, feats), BF16),
-        vmem((ROWS, feats), BF16),
         vmem((8, 2 * ROWS), F32),
         vmem((2, ROWS, feats), F32),
         vmem((2, HALO, feats), BF16),
         vmem((2, HALO, feats), BF16),
         vmem((2, BLOCK * big, feats), BF16),
-        vmem((2, BLOCK * big, feats), BF16),
+        vmem((2, 2 * BLOCK, feats), BF16),
         vmem((BLOCK, width), BF16),
         vmem((BLOCK, width), BF16),
         vmem((BLOCK, width), F32),
-        vmem((2, ROWS, feats), BF16),
-        vmem((BLOCK, width), BF16),
         dma((5,)),
-        dma((4,)),
         dma((2,)),
         dma((2,)),
         dma((n_seq - 1,)),
@@ -366,28 +436,45 @@
         dma((n_seq - 1,)),
         dma((n_seq - 1,)),
         dma((2,)),
+        dma((4,)),
+        dma((4,)),
+        dma((4,)),
+        dma((4,)),
+        vmem((2, BLOCK, feats), BF16),
+        vmem((2, BLOCK, feats), BF16),
+        vmem((4, 16, feats), BF16),
+        vmem((4, 16, feats), BF16),
     ]
     scratch += [vmem((2, BLOCK >> b, feats), BF16) for b in range(big)]
     scratch += [vmem((16, feats), BF16) for b in small]
     scratch += [vmem((2**b, 16, feats), BF16) for b in small]
     scratch += [vmem((8, 16, feats), BF16) for b in small]
-    scratch += [vmem((2**b, 16, feats), BF16) for b in small]
-    anywhere = pl.BlockSpec(memory_space=pl.ANY)
-    return pl.pallas_call(
+    scratch += [vmem((2**b // (2 if b == 3 else 1), 16, feats), BF16) for b in small]
+    in_hbm = pl.BlockSpec(memory_space=pltpu.HBM)
+    in_vmem = pl.BlockSpec(memory_space=pltpu.VMEM)
+    shapes = [
+        jax.ShapeDtypeStruct((BLOCK, width), BF16),
+        jax.ShapeDtypeStruct((ROWS, feats), BF16),
+        jax.ShapeDtypeStruct((ROWS, feats), BF16),
+        jax.ShapeDtypeStruct((ROWS, feats), BF16),
+    ]
+    results = pl.pallas_call(
         functools.partial(kernel, n_seq, levels),
-        out_shape=[
-            jax.ShapeDtypeStruct((BLOCK, width), BF16),
-            jax.ShapeDtypeStruct((ROWS, feats), BF16),
-            jax.ShapeDtypeStruct((ROWS, feats), BF16),
-            jax.ShapeDtypeStruct((ROWS, feats), BF16),
-        ],
-        in_specs=[anywhere] * 5,
-        out_specs=[anywhere] * 4,
+        out_shape=shapes,
+        in_specs=[in_hbm] * 5,
+        out_specs=[in_vmem] * 4,
         scratch_shapes=scratch,
         compiler_params=pltpu.CompilerParams(
-            collective_id=0, has_side_effects=True, vmem_limit_bytes=40 * 2**20
+            collective_id=0, has_side_effects=True, vmem_limit_bytes=63 * 2**20
         ),
     )(queries, keys, values, w_out, d_mixed)
+    return pl.pallas_call(
+        write_kernel,
+        out_shape=shapes,
+        in_specs=[in_vmem] * 4,
+        out_specs=[in_vmem] * 4,
+        compiler_params=pltpu.CompilerParams(vmem_limit_bytes=63 * 2**20),
+    )(*results)
 
 
 def solution(mesh):

time: 38 us -> 27.3 us (0.72)
  the two profiles are of different devices: /device:TPU:13 before, /device:TPU:0 now
where the time goes in v2:
time: 27.3 us; the launch traced here: 27.2 us
  Pallas kernels  26.5 us (97%)
  between operations  0.64 us (2%)
    pallas_call x1, Pallas kernels, on_device(): pl.pallas_call(functools.partial(kernel, n_seq, levels), out_shape=shapes...  24.7 us
    pallas_call x1, Pallas kernels, on_device(): pl.pallas_call(write_kernel, out_shape=shapes, in_specs=[in_vmem] * 4, ou...  1.89 us

profile of v2, /device:TPU:0, one launch (start us, length us, event | category | flops | bytes accessed | tf_op | source)
XLA Modules:
  0.0 27.2 jit_solution(4617962520567464327)
XLA Ops:
  0.6 24.7 %shard_map.84 = (bf16[64,1024]{1,0:T(8,128)(2,1)}, bf16[128,512]{1,0:T(8,128)(2,1)}, bf16[128,512]{1,0:T(8,128)(2,1)}, bf16[128,512]{1,0:T(8,128)(2,1)}) custom-call(bf16[128,512]{1,0:T(8,128)(2,1)} %refs_0_.1, bf16[128,512]{1,0:T(8,128)(2,1)} %refs_1_.1, bf16[128,512]{1,0:T(8,128)(2,1)} %refs_2_.1, bf16[512,1024]{1,0:T(8,128)(2,1)} %refs_3_.1, ...), custom_call_target="tpu_custom_call" | custom-call | tf_op jit(solution)/shard_map/pallas_call | solution.py:461
  25.3 1.9 %shard_map.85 = (bf16[64,1024]{1,0:T(8,128)(2,1)}, bf16[128,512]{1,0:T(8,128)(2,1)}, bf16[128,512]{1,0:T(8,128)(2,1)}, bf16[128,512]{1,0:T(8,128)(2,1)}) custom-call(bf16[64,1024]{1,0:T(8,128)(2,1)} %get-tuple-element.8.refs_0_, bf16[128,512]{1,0:T(8,128)(2,1)} %get-tuple-element.9.refs_1_, bf16[128,512]{1,0:T(8,128)(2,1)} %get-tuple-element.10.refs_2_, ...), custom_call_target="tpu_custom_call" | custom-call | tf_op jit(solution)/shard_map/pallas_call | solution.py:471

commit v3 on v2

--- a/solution.py
+++ b/solution.py
@@ -64,6 +64,7 @@
     hd = lax.axis_index("head")
     other_head = 1 - hd
     core = me % 2
+    part_of = (slice(0, feats // 2), slice(feats // 2, feats))
     twin = me + 1 - 2 * core
 
     loads = [
@@ -136,13 +137,13 @@
         pl.when(has_across)(lambda: pl.semaphore_wait(barrier, greeted + 1))
         pl.when(jnp.logical_not(has_across))(lambda: pl.semaphore_wait(barrier, greeted))
 
-    def halo_copy(way):
+    def halo_copy(way, h):
         if way == 0:
-            src, dst, to = kv.at[:, HALO + BLOCK : FAR], kv.at[:, 0:BLOCK], me + 1
-        else:
-            src, dst, to = kv.at[:, HALO : HALO + BLOCK], kv.at[:, BLOCK:HALO], me - 1
+            src, dst, to = kv.at[:, HALO + BLOCK : FAR, part_of[h]], kv.at[:, 0:BLOCK, part_of[h]], me + 1
+        else:
+            src, dst, to = kv.at[:, HALO : HALO + BLOCK, part_of[h]], kv.at[:, BLOCK:HALO, part_of[h]], me - 1
         return pltpu.make_async_remote_copy(
-            src, dst, halo_s.at[way], halo_r.at[way],
+            src, dst, halo_s.at[h, way], halo_r.at[h, way],
             device_id={"seq": to}, device_id_type=MESH,
         )
 
@@ -151,18 +152,21 @@
     def count(b):
         return 2 ** (b - 1) if b in relayed else 2**b
 
-    def key_rows(b, at, n):
-        return kv.at[:, pl.ds(pl.multiple_of(FAR + BLOCK * b + at, 16), n)]
-
-    def far_copy(b, dest, slot):
+    def key_rows(b, at, n, h):
+        return kv.at[:, pl.ds(pl.multiple_of(FAR + BLOCK * b + at, 16), n), part_of[h]]
+
+    def far_copy(b, dest, slot, h):
         size, rows, sibling, mine = spans[b]
         to = sibling + dest
         if b in relayed:
             slot = core * (size // 2) + slot
             to = sibling + 2 * dest + core
-        dst = key_rows(b, slot * rows, rows) if b < 3 else srecv[b - 3].at[slot]
+        if b < 3:
+            src, dst = psend[b].at[:, :, part_of[h]], key_rows(b, slot * rows, rows, h)
+        else:
+            src, dst = psend[b].at[:, part_of[h]], srecv[b - 3].at[slot, :, part_of[h]]
         return pltpu.make_async_remote_copy(
-            psend[b], dst, far_s.at[size - 1 + dest], far_r.at[size - 1 + slot],
+            src, dst, far_s.at[h, size - 1 + dest], far_r.at[h, size - 1 + slot],
             device_id={"seq": to}, device_id_type=MESH,
         )
 
@@ -171,55 +175,58 @@
 
     mine_of = [span[3] for span in spans]
 
-    def relay_copy(b, part):
+    def relay_copy(b, part, h):
         if b < 3:
-            ref = key_rows(b, part * (BLOCK // 2), BLOCK // 2)
-        else:
-            ref = srecv[0].at[pl.ds(part * 4, 4)]
+            ref = key_rows(b, part * (BLOCK // 2), BLOCK // 2, h)
+        else:
+            ref = srecv[0].at[pl.ds(part * 4, 4), :, part_of[h]]
         return pltpu.make_async_remote_copy(
-            ref, ref, relay_s.at[b], relay_r.at[b],
+            ref, ref, relay_s.at[h, b], relay_r.at[h, b],
             device_id={"seq": twin}, device_id_type=MESH,
         )
 
-    for b in reversed(range(levels)):
-        each(count(b), lambda i, b=b: far_copy(b, i, my_slot(b)).start())
-
     has_next = me < n_seq - 1
     has_prev = me > 0
-    pl.when(has_next)(lambda: halo_copy(0).start())
-    pl.when(has_prev)(lambda: halo_copy(1).start())
+    for h in range(2):
+        for b in reversed(range(levels)):
+            each(count(b), lambda i: far_copy(b, i, my_slot(b), h).start())
+        pl.when(has_next)(lambda: halo_copy(0, h).start())
+        pl.when(has_prev)(lambda: halo_copy(1, h).start())
 
     loads[2].wait()
     loads[3].wait()
     dattn[...] = dot_nt(dm[...], w[...]).astype(BF16)
     loads[4].wait()
 
-    pl.when(has_prev)(lambda: halo_copy(0).wait_recv())
-    pl.when(has_next)(lambda: halo_copy(1).wait_recv())
-    for b in range(levels):
-        each(count(b), lambda i, b=b: far_copy(b, 0, i).wait_recv())
-        if b in relayed:
-            relay_copy(b, core).start()
-    for b in relayed:
-        relay_copy(b, 1 - core).wait_recv()
+    def hand_on(h):
+        for b in reversed(relayed):
+            each(count(b), lambda i: far_copy(b, 0, i, h).wait_recv())
+            relay_copy(b, core, h).start()
 
     def place(b, slot):
         return (slot % 2) * 4 + slot // 2 if b == 3 else slot
 
-    for b in range(3, levels):
-        rows = spans[b][1]
-        per = 8 // rows
-        pieces = []
-        for g in range(8):
-            total = srecv[b - 3][place(b, g * per)].astype(F32)
-            for s in range(1, per):
-                total = total + srecv[b - 3][g * per + s].astype(F32)
-            pieces.append(total)
-        at = FAR + BLOCK * b
-        for part in range(2):
-            kv[part, at : at + BLOCK, :] = jnp.concatenate(
-                [piece[8 * part : 8 * part + 8] for piece in pieces], axis=0
-            ).astype(BF16)
+    def collect(h):
+        pl.when(has_prev)(lambda: halo_copy(0, h).wait_recv())
+        pl.when(has_next)(lambda: halo_copy(1, h).wait_recv())
+        for b in range(levels):
+            if b in relayed:
+                relay_copy(b, 1 - core, h).wait_recv()
+            else:
+                each(count(b), lambda i: far_copy(b, 0, i, h).wait_recv())
+        for b in range(3, levels):
+            per = 8 // spans[b][1]
+            pieces = []
+            for g in range(8):
+                total = srecv[b - 3][place(b, g * per), :, part_of[h]].astype(F32)
+                for s in range(1, per):
+                    total = total + srecv[b - 3][g * per + s, :, part_of[h]].astype(F32)
+                pieces.append(total)
+            at = FAR + BLOCK * b
+            for part in range(2):
+                kv[part, at : at + BLOCK, part_of[h]] = jnp.concatenate(
+                    [piece[8 * part : 8 * part + 8] for piece in pieces], axis=0
+                ).astype(BF16)
 
     lane = lax.broadcasted_iota(jnp.int32, (1, PAIR), 1)
     head_a = jnp.where(lane < HEAD_DIM, 1.0, 0.0).astype(BF16)
@@ -229,7 +236,7 @@
     mask0 = jnp.where(first, 1.0, 0.0)
     mask1 = jnp.where(first, 0.0, 1.0)
 
-    for pair in range(feats // PAIR):
+    def attend(pair):
         cols = slice(pair * PAIR, (pair + 1) * PAIR)
         qp = q[:, cols] * jnp.asarray(0.125, BF16)
         dap = dattn[:, cols]
@@ -281,68 +288,89 @@
                     [grad[at + 8 * g : at + 8 * g + 8] for grad in grads], axis=0
                 ).astype(BF16)
 
-    def ghalo_copy(way):
+    def ghalo_copy(way, h):
         if way == 0:
-            src, dst, to = hsend.at[:, 0:BLOCK], hrecv.at[:, BLOCK:HALO], me - 1
-        else:
-            src, dst, to = hsend.at[:, BLOCK:HALO], hrecv.at[:, 0:BLOCK], me + 1
+            src, dst, to = hsend.at[:, 0:BLOCK, part_of[h]], hrecv.at[:, BLOCK:HALO, part_of[h]], me - 1
+        else:
+            src, dst, to = hsend.at[:, BLOCK:HALO, part_of[h]], hrecv.at[:, 0:BLOCK, part_of[h]], me + 1
         return pltpu.make_async_remote_copy(
-            src, dst, ghalo_s.at[way], ghalo_r.at[way],
+            src, dst, ghalo_s.at[h, way], ghalo_r.at[h, way],
             device_id={"seq": to}, device_id_type=MESH,
         )
 
-    def sum_copy(b):
+    def sum_copy(b, h):
         half = BLOCK // 2
         if b < 3:
             at = BLOCK * b + (1 - core) * half
-            src = gsend.at[:, pl.ds(pl.multiple_of(at, half), half)]
-            dst = sum_recv.at[:, half * (b - 1) : half * b]
-        else:
-            src = gssend[0].at[pl.ds((1 - core) * 4, 4)]
-            dst = small_recv
+            src = gsend.at[:, pl.ds(pl.multiple_of(at, half), half), part_of[h]]
+            dst = sum_recv.at[:, half * (b - 1) : half * b, part_of[h]]
+        else:
+            src = gssend[0].at[pl.ds((1 - core) * 4, 4), :, part_of[h]]
+            dst = small_recv.at[:, :, part_of[h]]
         return pltpu.make_async_remote_copy(
-            src, dst, sum_s.at[b], sum_r.at[b],
+            src, dst, sum_s.at[h, b], sum_r.at[h, b],
             device_id={"seq": twin}, device_id_type=MESH,
         )
 
-    def gfar_copy(b, dest, slot):
+    def gfar_copy(b, dest, slot, h):
         size, rows, sibling, mine = spans[b]
         to = sibling + dest
         if b == 0:
-            src, dst = gsend.at[:, 0:BLOCK], grecv.at[:, 0:BLOCK]
+            src, dst = gsend.at[:, 0:BLOCK, part_of[h]], grecv.at[:, 0:BLOCK, part_of[h]]
         elif b < 3:
             half = BLOCK // 2
-            src = sum_send.at[:, pl.ds(pl.multiple_of(half * (b - 1) + dest * rows, 16), rows)]
-            dst = grecv.at[:, pl.ds(pl.multiple_of(half * (b + 1) + slot * rows, 16), rows)]
+            src = sum_send.at[:, pl.ds(pl.multiple_of(half * (b - 1) + dest * rows, 16), rows), part_of[h]]
+            dst = grecv.at[:, pl.ds(pl.multiple_of(half * (b + 1) + slot * rows, 16), rows), part_of[h]]
         elif b == 3:
-            src, dst = small_send.at[dest], gsrecv[0].at[slot]
-        else:
-            src = gssend[b - 3].at[dest // (8 // rows)]
-            dst = gsrecv[b - 3].at[slot]
+            src, dst = small_send.at[dest, :, part_of[h]], gsrecv[0].at[slot, :, part_of[h]]
+        else:
+            src = gssend[b - 3].at[dest // (8 // rows), :, part_of[h]]
+            dst = gsrecv[b - 3].at[slot, :, part_of[h]]
         if b in relayed:
             to = sibling + 2 * dest + core
         return pltpu.make_async_remote_copy(
-            src, dst, gfar_s.at[size - 1 + dest], gfar_r.at[size - 1 + slot],
+            src, dst, gfar_s.at[h, size - 1 + dest], gfar_r.at[h, size - 1 + slot],
             device_id={"seq": to}, device_id_type=MESH,
         )
 
-    for b in reversed(relayed):
-        sum_copy(b).start()
-    pl.when(has_prev)(lambda: ghalo_copy(0).start())
-    pl.when(has_next)(lambda: ghalo_copy(1).start())
-    for b in reversed(range(levels)):
-        if b in relayed:
-            sum_copy(b).wait_recv()
-            half = BLOCK // 2
+    def give_back(h):
+        for b in reversed(relayed):
+            sum_copy(b, h).start()
+        pl.when(has_prev)(lambda: ghalo_copy(0, h).start())
+        pl.when(has_next)(lambda: ghalo_copy(1, h).start())
+        for b in range(levels):
+            if b not in relayed:
+                each(count(b), lambda i: gfar_copy(b, i, my_slot(b), h).start())
+
+    def give_back_sums(h):
+        half = BLOCK // 2
+        for b in reversed(relayed):
+            sum_copy(b, h).wait_recv()
             if b < 3:
                 mine_rows = pl.ds(pl.multiple_of(BLOCK * b + core * half, half), half)
-                own = gsend[:, mine_rows, :].astype(F32)
-                both_cores = own + sum_recv[:, half * (b - 1) : half * b, :].astype(F32)
-                sum_send[:, half * (b - 1) : half * b, :] = both_cores.astype(BF16)
+                own = gsend[:, mine_rows, part_of[h]].astype(F32)
+                theirs = sum_recv[:, half * (b - 1) : half * b, part_of[h]].astype(F32)
+                sum_send[:, half * (b - 1) : half * b, part_of[h]] = (own + theirs).astype(BF16)
             else:
-                own = gssend[0][pl.ds(core * 4, 4)].astype(F32)
-                small_send[...] = (own + small_recv[...].astype(F32)).astype(BF16)
-        each(count(b), lambda i, b=b: gfar_copy(b, i, my_slot(b)).start())
+                own = gssend[0][pl.ds(core * 4, 4), :, part_of[h]].astype(F32)
+                theirs = small_recv[:, :, part_of[h]].astype(F32)
+                small_send[:, :, part_of[h]] = (own + theirs).astype(BF16)
+            each(count(b), lambda i: gfar_copy(b, i, my_slot(b), h).start())
+
+    pairs = feats // PAIR // 2
+    hand_on(0)
+    collect(0)
+    for pair in range(pairs):
+        attend(pair)
+        if pair == 0:
+            hand_on(1)
+    give_back(0)
+    collect(1)
+    for pair in range(pairs, 2 * pairs):
+        attend(pair)
+        if pair == pairs:
+            give_back_sums(0)
+    give_back(1)
 
     theirs = pl.ds(pl.multiple_of(other_head * BLOCK, BLOCK), BLOCK)
     ours = pl.ds(pl.multiple_of(hd * BLOCK, BLOCK), BLOCK)
@@ -352,47 +380,46 @@
         device_id={"head": other_head}, device_id_type=MESH,
     )
     mix_copy.start()
+    give_back_sums(1)
     mix_own[...] = dot_nn(attn[ours, :], w[...])
 
-    pl.when(has_next)(lambda: ghalo_copy(0).wait_recv())
-    pl.when(has_prev)(lambda: ghalo_copy(1).wait_recv())
-    for b in range(levels):
-        each(count(b), lambda i, b=b: gfar_copy(b, 0, i).wait_recv())
-
-    for part in range(2):
-        total = gown[part] + hrecv[part].astype(F32)
-        for b, (size, rows, sibling, mine) in enumerate(spans):
-            if b < 3:
-                wide = rows * count(b)
-                at = BLOCK // 2 * (b + 1) if b else 0
+    for h in range(2):
+        pl.when(has_next)(lambda: ghalo_copy(0, h).wait_recv())
+        pl.when(has_prev)(lambda: ghalo_copy(1, h).wait_recv())
+        for b in range(levels):
+            each(count(b), lambda i: gfar_copy(b, 0, i, h).wait_recv())
+        for part in range(2):
+            total = gown[part, :, part_of[h]] + hrecv[part, :, part_of[h]].astype(F32)
+            for b, (size, rows, sibling, mine) in enumerate(spans):
+                group = ROWS // rows
+                wide = (rows if b < 3 else 16) * count(b)
                 token = lax.broadcasted_iota(jnp.int32, (ROWS, wide), 0)
                 row = lax.broadcasted_iota(jnp.int32, (ROWS, wide), 1)
-                group = ROWS // rows
-                mat = jnp.where(token // group == row % rows, 1.0 / group, 0.0).astype(BF16)
-                total = total + dot_nn(mat, grecv[part, at : at + wide, :])
-            else:
-                wide = 16 * count(b)
-                token = lax.broadcasted_iota(jnp.int32, (ROWS, wide), 0)
-                row = lax.broadcasted_iota(jnp.int32, (ROWS, wide), 1) % 16
-                group = ROWS // rows
-                wanted = token // group + (mine * rows) % 8 + 8 * part
-                mat = jnp.where(wanted == row, 1.0 / group, 0.0).astype(BF16)
-                total = total + dot_nn(mat, gsrecv[b - 3][...].reshape(wide, feats))
-        (dk_out, dv_out)[part][...] = total.astype(BF16)
+                if b < 3:
+                    at = BLOCK // 2 * (b + 1) if b else 0
+                    same = token // group == row % rows
+                    got = grecv[part, at : at + wide, part_of[h]]
+                else:
+                    same = token // group + (mine * rows) % 8 + 8 * part == row % 16
+                    got = gsrecv[b - 3][:, :, part_of[h]].reshape(wide, feats // 2)
+                mat = jnp.where(same, 1.0 / group, 0.0).astype(BF16)
+                total = total + dot_nn(mat, got)
+            (dk_out, dv_out)[part][:, part_of[h]] = total.astype(BF16)
 
     mix_copy.wait_recv()
     mixed_out[...] = (mix_own[...] + mix_recv[...].astype(F32)).astype(BF16)
 
-    pl.when(has_next)(lambda: halo_copy(0).wait_send())
-    pl.when(has_prev)(lambda: halo_copy(1).wait_send())
-    pl.when(has_prev)(lambda: ghalo_copy(0).wait_send())
-    pl.when(has_next)(lambda: ghalo_copy(1).wait_send())
-    for b in range(levels):
-        each(count(b), lambda i, b=b: far_copy(b, i, my_slot(b)).wait_send())
-        each(count(b), lambda i, b=b: gfar_copy(b, i, my_slot(b)).wait_send())
-    for b in relayed:
-        relay_copy(b, core).wait_send()
-        sum_copy(b).wait_send()
+    for h in range(2):
+        pl.when(has_next)(lambda: halo_copy(0, h).wait_send())
+        pl.when(has_prev)(lambda: halo_copy(1, h).wait_send())
+        pl.when(has_prev)(lambda: ghalo_copy(0, h).wait_send())
+        pl.when(has_next)(lambda: ghalo_copy(1, h).wait_send())
+        for b in range(levels):
+            each(count(b), lambda i: far_copy(b, i, my_slot(b), h).wait_send())
+            each(count(b), lambda i: gfar_copy(b, i, my_slot(b), h).wait_send())
+        for b in relayed:
+            relay_copy(b, core, h).wait_send()
+            sum_copy(b, h).wait_send()
     mix_copy.wait_send()
 
 
@@ -427,19 +454,19 @@
         vmem((BLOCK, width), BF16),
         vmem((BLOCK, width), F32),
         dma((5,)),
+        dma((2, 2)),
+        dma((2, 2)),
+        dma((2, n_seq - 1)),
+        dma((2, n_seq - 1)),
+        dma((2, 2)),
+        dma((2, 2)),
+        dma((2, n_seq - 1)),
+        dma((2, n_seq - 1)),
         dma((2,)),
-        dma((2,)),
-        dma((n_seq - 1,)),
-        dma((n_seq - 1,)),
-        dma((2,)),
-        dma((2,)),
-        dma((n_seq - 1,)),
-        dma((n_seq - 1,)),
-        dma((2,)),
-        dma((4,)),
-        dma((4,)),
-        dma((4,)),
-        dma((4,)),
+        dma((2, 4)),
+        dma((2, 4)),
+        dma((2, 4)),
+        dma((2, 4)),
         vmem((2, BLOCK, feats), BF16),
         vmem((2, BLOCK, feats), BF16),
         vmem((4, 16, feats), BF16),

time: 27.3 us -> 26 us (0.952)
  Pallas kernels: 26.5 us -> 25.2 us
    pallas_call x1, Pallas kernels: 24.7 us -> 23.3 us  [on_device(): pl.pallas_call(functools.partial(kernel, n_seq, levels), out_shape=shapes...]
where the time goes in v3:
time: 26 us; the launch traced here: 25.8 us
  Pallas kernels  25.2 us (97%)
  between operations  0.64 us (2%)
    pallas_call x1, Pallas kernels, on_device(): pl.pallas_call(functools.partial(kernel, n_seq, levels), out_shape=shapes...  23.3 us
    pallas_call x1, Pallas kernels, on_device(): pl.pallas_call(write_kernel, out_shape=shapes, in_specs=[in_vmem] * 4, ou...  1.89 us

profile of v3, /device:TPU:0, one launch (start us, length us, event | category | flops | bytes accessed | tf_op | source)
XLA Modules:
  0.0 25.8 jit_solution(10506703938053623778)
XLA Ops:
  0.6 23.3 %shard_map.84 = (bf16[64,1024]{1,0:T(8,128)(2,1)}, bf16[128,512]{1,0:T(8,128)(2,1)}, bf16[128,512]{1,0:T(8,128)(2,1)}, bf16[128,512]{1,0:T(8,128)(2,1)}) custom-call(bf16[128,512]{1,0:T(8,128)(2,1)} %refs_0_.1, bf16[128,512]{1,0:T(8,128)(2,1)} %refs_1_.1, bf16[128,512]{1,0:T(8,128)(2,1)} %refs_2_.1, bf16[512,1024]{1,0:T(8,128)(2,1)} %refs_3_.1, ...), custom_call_target="tpu_custom_call" | custom-call | tf_op jit(solution)/shard_map/pallas_call | solution.py:488
  23.9 1.9 %shard_map.85 = (bf16[64,1024]{1,0:T(8,128)(2,1)}, bf16[128,512]{1,0:T(8,128)(2,1)}, bf16[128,512]{1,0:T(8,128)(2,1)}, bf16[128,512]{1,0:T(8,128)(2,1)}) custom-call(bf16[64,1024]{1,0:T(8,128)(2,1)} %get-tuple-element.8.refs_0_, bf16[128,512]{1,0:T(8,128)(2,1)} %get-tuple-element.9.refs_1_, bf16[128,512]{1,0:T(8,128)(2,1)} %get-tuple-element.10.refs_2_, ...), custom_call_target="tpu_custom_call" | custom-call | tf_op jit(solution)/shard_map/pallas_call | solution.py:498

commit v4 on v3

--- a/solution.py
+++ b/solution.py
@@ -424,8 +424,16 @@
 
 
 def write_kernel(*refs):
-    for i in range(4):
-        refs[4 + i][...] = refs[i][...]
+    in_sem, out_sem = refs[12:]
+    reads = [pltpu.make_async_copy(refs[i], refs[8 + i], in_sem.at[i]) for i in range(4)]
+    writes = [pltpu.make_async_copy(refs[8 + i], refs[4 + i], out_sem.at[i]) for i in range(4)]
+    for read in reads:
+        read.start()
+    for read, write in zip(reads, writes):
+        read.wait()
+        write.start()
+    for write in writes:
+        write.wait()
 
 
 def on_device(n_seq, queries, keys, values, w_out, d_mixed):
@@ -498,8 +506,9 @@
     return pl.pallas_call(
         write_kernel,
         out_shape=shapes,
-        in_specs=[in_vmem] * 4,
-        out_specs=[in_vmem] * 4,
+        in_specs=[in_hbm] * 4,
+        out_specs=[in_hbm] * 4,
+        scratch_shapes=[vmem(s.shape, s.dtype) for s in shapes] + [dma((4,)), dma((4,))],
         compiler_params=pltpu.CompilerParams(vmem_limit_bytes=63 * 2**20),
     )(*results)
 

time: 26 us -> 25.9 us (level)
  no operation moved by 1% of the time
where the time goes in v4:
time: 25.9 us; the launch traced here: 25.7 us
  Pallas kernels  25.1 us (97%)
  between operations  0.64 us (2%)
    pallas_call x1, Pallas kernels, on_device(): pl.pallas_call(functools.partial(kernel, n_seq, levels), out_shape=shapes...  23.3 us
    pallas_call x1, Pallas kernels, on_device(): pl.pallas_call(write_kernel, out_shape=shapes, in_specs=[in_hbm] * 4, out...  1.82 us

profile of v4, /device:TPU:0, one launch (start us, length us, event | category | flops | bytes accessed | tf_op | source)
XLA Modules:
  0.0 25.7 jit_solution(12876991661911633728)
XLA Ops:
  0.6 23.3 %shard_map.84 = (bf16[64,1024]{1,0:T(8,128)(2,1)}, bf16[128,512]{1,0:T(8,128)(2,1)}, bf16[128,512]{1,0:T(8,128)(2,1)}, bf16[128,512]{1,0:T(8,128)(2,1)}) custom-call(bf16[128,512]{1,0:T(8,128)(2,1)} %refs_0_.1, bf16[128,512]{1,0:T(8,128)(2,1)} %refs_1_.1, bf16[128,512]{1,0:T(8,128)(2,1)} %refs_2_.1, bf16[512,1024]{1,0:T(8,128)(2,1)} %refs_3_.1, ...), custom_call_target="tpu_custom_call" | custom-call | tf_op jit(solution)/shard_map/pallas_call | solution.py:496
  23.9 1.8 %shard_map.85 = (bf16[64,1024]{1,0:T(8,128)(2,1)}, bf16[128,512]{1,0:T(8,128)(2,1)}, bf16[128,512]{1,0:T(8,128)(2,1)}, bf16[128,512]{1,0:T(8,128)(2,1)}) custom-call(bf16[64,1024]{1,0:T(8,128)(2,1)} %get-tuple-element.8.refs_0_, bf16[128,512]{1,0:T(8,128)(2,1)} %get-tuple-element.9.refs_1_, bf16[128,512]{1,0:T(8,128)(2,1)} %get-tuple-element.10.refs_2_, ...), custom_call_target="tpu_custom_call" | custom-call | tf_op jit(solution)/shard_map/pallas_call | solution.py:506
